TPU v7x, 32 devices: a whole 2x2x4 slice. The times are simulated.
32 devices in a mesh: task: 4 (over x, core), dp: 8 (over z, y).
Axes of the slice: x: 2, y: 2, z: 4, core: 2. Of those that a mesh axis runs over, the one named last changes fastest.
Arguments:
- features: bfloat16 [16, 36, 48, 512], P('dp'), may hold values from -6 to 6
- labels: int32 [16, 36, 48], P('dp'), may hold values from 0 to 12
- depth_mask: int32 [16, 36, 48], P('dp'), may hold values 0 or 1
- depth_target: float32 [16, 36, 48], P('dp'), may hold values from 0.5 to 3
- normal_target: float32 [16, 3, 36, 48], P('dp'), may hold values from -1 to 1
- scene_ids: int32 [16], P('dp'), may hold values from 0 to 26
- task_weights: float32 [27, 4], replicated, may hold values from 0.5 to 2
- conflict: int32 [4, 4], replicated, may hold values 0 or 1
- trunk_copy: bfloat16 [2, 9, 512, 512], P(None, None, 'dp'), may hold values from -0.09375 to 0.09375
- trunk_master: float32 [2, 9, 512, 512], P(None, None, 'dp'), may hold values from -0.09375 to 0.09375
- trunk_left: float32 [2, 9, 512, 512], P(None, None, 'dp')
- trunk_right: float32 [2, 9, 512, 512], P(None, None, 'dp')
- left_root: float32 [2, 9, 512, 512], P(None, None, 'dp')
- right_root: float32 [2, 9, 512, 512], replicated
- head_copy: bfloat16 [4, 2, 512, 256], P('task', None, 'dp'), may hold values from -0.25 to 0.25
- head_master: float32 [4, 2, 512, 256], P('task', None, 'dp'), may hold values from -0.25 to 0.25
- head_first: float32 [4, 2, 512, 256], P('task', None, 'dp'), may hold values from -0.09375 to 0.09375
- head_second: float32 [4, 2, 512, 256], P('task', None, 'dp'), may hold values from 3.616898e-05 to 0.00014467593
- out_copy: bfloat16 [256, 18], replicated, may hold values from -0.375 to 0.375
- out_master: float32 [256, 18], replicated, may hold values from -0.375 to 0.375
- out_first: float32 [256, 18], replicated, may hold values from -0.09375 to 0.09375
- out_second: float32 [256, 18], replicated, may hold values from 3.616898e-05 to 0.00014467593
- trunk_gains: float32 [4, 512], replicated, may hold values from 0.5 to 1.5
- gains_first: float32 [4, 512], replicated, may hold values from -0.09375 to 0.09375
- gains_second: float32 [4, 512], replicated, may hold values from 3.616898e-05 to 0.00014467593
- head_bias: float32 [4, 256], replicated, may hold values from -3 to 3
- bias_first: float32 [4, 256], replicated, may hold values from -0.09375 to 0.09375
- bias_second: float32 [4, 256], replicated, may hold values from 3.616898e-05 to 0.00014467593
Outputs:
- trunk_grad: float32 [2, 9, 512, 512], P(None, None, 'dp')
- left_new: float32 [2, 9, 512, 512], P(None, None, 'dp')
- right_new: float32 [2, 9, 512, 512], P(None, None, 'dp')
- trunk_master_new: float32 [2, 9, 512, 512], P(None, None, 'dp')
- trunk_copy_new: bfloat16 [2, 9, 512, 512], P(None, None, 'dp')
- head_first_new: float32 [4, 2, 512, 256], P('task', None, 'dp')
- head_second_new: float32 [4, 2, 512, 256], P('task', None, 'dp')
- head_master_new: float32 [4, 2, 512, 256], P('task', None, 'dp')
- head_copy_new: bfloat16 [4, 2, 512, 256], P('task', None, 'dp')
- out_first_new: float32 [256, 18], replicated
- out_second_new: float32 [256, 18], replicated
- out_master_new: float32 [256, 18], replicated
- out_copy_new: bfloat16 [256, 18], replicated
- gains_first_new: float32 [4, 512], replicated
- gains_second_new: float32 [4, 512], replicated
- trunk_gains_new: float32 [4, 512], replicated
- bias_first_new: float32 [4, 256], replicated
- bias_second_new: float32 [4, 256], replicated
- head_bias_new: float32 [4, 256], replicated
- loss_terms: float32 [5], replicated
- pair_products: float32 [4, 4], replicated
All inputs are finite; a program needn't handle non-finite values. No bound on the sum of `depth_mask` on one device may be relied on, other than what follows from the above.
Results may differ from a plain program's by a relative error of at most 0.0055.
Values may be sent and summed in bfloat16 or wider, within the bound.
A program may use at most 320 MiB of HBM per device.

v0:
```python
import jax
import jax.numpy as jnp
from jax import lax
from jax.sharding import PartitionSpec as P

BRANCH_WIDTH = 256
CLASSES = 13
TASKS = 4
DILATION_STEP = 2
STEP = 5


PRECISE = lax.Precision.HIGHEST
NORM_EPS = 1e-05
RATE_TRUNK = 0.3
RATE_MATRIX = 0.05
RATE_VECTOR = 0.3
WEIGHT_DECAY = 0.01
ADAM_EPS = 1e-08
GRAM_EPS = 1e-12
CONTRACT_ROWS = (((0,), (0,)), ((), ()))
CONTRACT_COLS = (((1,), (1,)), ((), ()))


def silu_slope(tap_values):
    sigmoid = jax.nn.sigmoid(tap_values)
    return sigmoid * (1.0 + tap_values * (1.0 - sigmoid))


def tap_pieces(tap_values, transposed):
    images, feature_rows, feature_columns, inner_width = tap_values.shape
    padded_input = jnp.pad(
        tap_values, ((0, 0), (DILATION_STEP, DILATION_STEP), (DILATION_STEP, DILATION_STEP), (0, 0))
    )
    pieces = []
    for tap_index in range(9):
        kernel_row, kernel_column = divmod(tap_index, 3)
        if transposed:
            kernel_row, kernel_column = (2 - kernel_row, 2 - kernel_column)
        shifted_window = padded_input[
            :,
            DILATION_STEP * kernel_row : DILATION_STEP * kernel_row + feature_rows,
            DILATION_STEP * kernel_column : DILATION_STEP * kernel_column + feature_columns,
            :,
        ]
        pieces.append(shifted_window.reshape(-1, inner_width))
    return pieces


def conv_taps(tap_values, weights, transposed):
    contract = CONTRACT_COLS if transposed else (((1,), (0,)), ((), ()))
    result = None
    for tap_index, shifted_window in enumerate(tap_pieces(tap_values, transposed)):
        partial_sum = lax.dot_general(
            shifted_window, weights[tap_index], contract, preferred_element_type=jnp.float32
        )
        result = partial_sum if result is None else result + partial_sum
    return result


def conv_weight_grad(tap_values, delta_rows):
    return jnp.stack(
        [
            lax.dot_general(
                shifted_window, delta_rows, CONTRACT_ROWS, preferred_element_type=jnp.float32
            )
            for shifted_window in tap_pieces(tap_values, False)
        ]
    )


def norm_forward(conv_out, gain, shift, pixels):
    totals = lax.psum((jnp.sum(conv_out, axis=0), jnp.sum(conv_out * conv_out, axis=0)), "dp")
    center = totals[0] / pixels
    inverse = lax.rsqrt(totals[1] / pixels - center * center + NORM_EPS)
    centered = (conv_out - center) * inverse
    return (gain * centered + shift, centered, inverse)


def norm_backward(upstream, centered, inverse, gain, pixels):
    totals = lax.psum((jnp.sum(upstream, axis=0), jnp.sum(upstream * centered, axis=0)), "dp")
    result = gain * inverse * (upstream - totals[0] / pixels - centered * (totals[1] / pixels))
    return (result, totals[1], totals[0])


def boundary(labels):
    across = jnp.pad(
        (labels[:, :, 1:] != labels[:, :, :-1]).astype(jnp.float32), ((0, 0), (0, 0), (0, 1))
    )
    downward = jnp.pad(
        (labels[:, 1:, :] != labels[:, :-1, :]).astype(jnp.float32), ((0, 0), (0, 1), (0, 0))
    )
    return jnp.maximum(across, downward)


def pixel_data(labels, depth_mask, depth_target, normal_target, scene_ids, task_weights):
    images, feature_rows, feature_columns = labels.shape
    choose = (scene_ids[:, None] == jnp.arange(task_weights.shape[0])[None, :]).astype(jnp.float32)
    per_image = jnp.dot(choose, task_weights, precision=PRECISE)
    return (
        labels.reshape(-1),
        depth_mask.reshape(-1).astype(jnp.float32),
        boundary(labels).reshape(-1),
        depth_target.reshape(-1),
        jnp.transpose(normal_target, (0, 2, 3, 1)).reshape(-1, 3),
        jnp.repeat(per_image, feature_rows * feature_columns, axis=0),
    )


def task_sums(logits, pixel_info):
    labels, valid_mask, edge_target, depth_values, normals, weights = pixel_info
    classes = logits[:, :CLASSES]
    largest = jnp.max(classes, axis=1, keepdims=True)
    spread = jnp.log(jnp.sum(jnp.exp(classes - largest), axis=1)) + largest[:, 0]
    picked = jnp.sum(
        jnp.where(labels[:, None] == jnp.arange(CLASSES)[None, :], classes, 0.0), axis=1
    )
    segment = jnp.sum(weights[:, 0] * (spread - picked))
    offset = logits[:, CLASSES] - depth_values
    distance = jnp.sum(weights[:, 1] * valid_mask * (jnp.sqrt(offset * offset + 1.0) - 1.0))
    predicted = logits[:, CLASSES + 1 : CLASSES + 4]
    cosine = jnp.sum(predicted * normals, axis=1) * lax.rsqrt(
        (jnp.sum(predicted * predicted, axis=1) + 1.0) * (jnp.sum(normals * normals, axis=1) + 1.0)
    )
    surface = jnp.sum(weights[:, 2] * (1.0 - cosine))
    edge_logit = logits[:, CLASSES + 4]
    contour = jnp.sum(weights[:, 3] * (jax.nn.softplus(edge_logit) - edge_target * edge_logit))
    return jnp.stack([segment, distance, surface, contour])


def combine_weights(pair_products, conflict):
    offdiagonal = (1.0 - jnp.eye(TASKS, dtype=jnp.float32)) * conflict.astype(jnp.float32)
    ratios = offdiagonal * pair_products / (jnp.diagonal(pair_products)[None, :] + GRAM_EPS)
    return 1.0 - jnp.sum(ratios, axis=0)


def adamw_update(gradient, moment_one, moment_two, weight, rate):
    moment_one = 0.5 * moment_one + 0.5 * gradient
    moment_two = 0.5 * moment_two + 0.5 * gradient * gradient
    correction = 1.0 - 0.5**STEP
    weight = weight - rate * (
        moment_one / correction / (jnp.sqrt(moment_two / correction) + ADAM_EPS)
        + WEIGHT_DECAY * weight
    )
    return (moment_one, moment_two, weight)


def mixed_gradient(every_task, divisor):
    scaled = every_task / divisor[:, None, None, None, None]
    flattened = scaled.reshape(TASKS, -1)
    return (scaled, jnp.dot(flattened, flattened.T, precision=PRECISE))


def body(
    features,
    labels,
    depth_mask,
    depth_target,
    normal_target,
    scene_ids,
    task_weights,
    conflict,
    trunk_copy,
    trunk_master,
    trunk_left,
    trunk_right,
    left_root,
    right_root,
    head_copy,
    head_master,
    head_first,
    head_second,
    out_copy,
    out_master,
    out_first,
    out_second,
    trunk_gains,
    gains_first,
    gains_second,
    head_bias,
    bias_first,
    bias_second,
):
    images, feature_rows, feature_columns, channels = features.shape
    pixels = jnp.array(images * feature_rows * feature_columns * lax.axis_size("dp"), jnp.float32)
    task_index = lax.axis_index("task")
    owner_index = lax.axis_index("dp")
    shard_rows = trunk_copy.shape[2]
    trunk_full, head_full = (
        lax.all_gather(trunk_copy, "dp", axis=2, tiled=True),
        lax.all_gather(head_copy, "dp", axis=2, tiled=True),
    )
    pixel_info = pixel_data(
        labels, depth_mask, depth_target, normal_target, scene_ids, task_weights
    )
    local_valid = jnp.sum(pixel_info[1])
    valid_count = lax.psum(local_valid, "dp")
    first_conv = conv_taps(features, trunk_full[0], False)
    first_norm, first_center, first_scale = norm_forward(
        first_conv, trunk_gains[0], trunk_gains[1], pixels
    )
    first_act = (
        jax.nn.silu(first_norm)
        .astype(jnp.bfloat16)
        .reshape(images, feature_rows, feature_columns, channels)
    )
    second_conv = conv_taps(first_act, trunk_full[1], False)
    second_norm, second_center, second_scale = norm_forward(
        second_conv, trunk_gains[2], trunk_gains[3], pixels
    )
    residual_in = second_norm + features.reshape(-1, channels)
    trunk_out = jax.nn.silu(residual_in).astype(jnp.bfloat16)
    pooled = jnp.mean(trunk_out.reshape(images, -1, channels), axis=1, dtype=jnp.float32).astype(
        jnp.bfloat16
    )
    selector = (jnp.arange(TASKS) == task_index).astype(jnp.float32)
    own_bias = jnp.dot(selector, head_bias, precision=PRECISE)
    head_pre = jnp.dot(trunk_out, head_full[0, 0], preferred_element_type=jnp.float32).reshape(
        images, -1, BRANCH_WIDTH
    )
    head_pre = (
        head_pre
        + jnp.dot(pooled, head_full[0, 1], preferred_element_type=jnp.float32)[:, None, :]
        + own_bias
    )
    head_pre = head_pre.reshape(-1, BRANCH_WIDTH)
    hidden_act = jax.nn.silu(head_pre).astype(jnp.bfloat16)
    logits = jnp.dot(hidden_act, out_copy, preferred_element_type=jnp.float32)
    totals, pullback = jax.vjp(lambda tap_values: task_sums(tap_values, pixel_info), logits)
    logit_grad = pullback(selector)[0].astype(jnp.bfloat16)
    out_grad = lax.dot_general(
        hidden_act, logit_grad, CONTRACT_ROWS, preferred_element_type=jnp.float32
    )
    hidden_grad = lax.dot_general(
        logit_grad, out_copy, CONTRACT_COLS, preferred_element_type=jnp.float32
    )
    pre_grad = (hidden_grad * silu_slope(head_pre)).astype(jnp.bfloat16)
    bias_grad = jnp.sum(pre_grad, axis=0, dtype=jnp.float32)
    per_image = jnp.sum(pre_grad.reshape(images, -1, BRANCH_WIDTH), axis=1, dtype=jnp.float32)
    input_grad = lax.dot_general(
        trunk_out, pre_grad, CONTRACT_ROWS, preferred_element_type=jnp.float32
    )
    pool_grad = jnp.dot(pooled.astype(jnp.float32).T, per_image, precision=PRECISE)
    pooled_back = jnp.dot(per_image, head_full[0, 1].astype(jnp.float32).T, precision=PRECISE)
    out_back = lax.dot_general(
        pre_grad, head_full[0, 0], CONTRACT_COLS, preferred_element_type=jnp.float32
    )
    out_back = (
        out_back.reshape(images, -1, channels)
        + pooled_back[:, None, :] / (feature_rows * feature_columns)
    ).reshape(-1, channels)
    second_grad = out_back * silu_slope(residual_in)
    second_back, second_gain, second_shift = norm_backward(
        second_grad, second_center, second_scale, trunk_gains[2], pixels
    )
    second_back = second_back.astype(jnp.bfloat16)
    second_weight = conv_weight_grad(first_act, second_back)
    act_grad = conv_taps(
        second_back.reshape(images, feature_rows, feature_columns, channels), trunk_full[1], True
    )
    first_grad = act_grad * silu_slope(first_norm)
    first_back, first_gain, first_shift = norm_backward(
        first_grad, first_center, first_scale, trunk_gains[0], pixels
    )
    first_weight = conv_weight_grad(features, first_back.astype(jnp.bfloat16))
    task_grad = jnp.stack([first_weight, second_weight])
    head_grad = jnp.stack([input_grad, pool_grad])[None]
    leading = (owner_index == 0).astype(jnp.float32)
    gains_part = (
        selector[:, None, None]
        * (leading * jnp.stack([first_gain, first_shift, second_gain, second_shift]))[None]
    )
    bias_part = selector[:, None] * bias_grad[None]
    loss_part = totals * selector
    gains_sum, bias_sum, out_sum, loss_sum = lax.psum(
        (gains_part, bias_part, out_grad, loss_part), ("task", "dp")
    )
    divisor = jnp.stack([pixels, valid_count, pixels, pixels])
    own_divisor = jnp.sum(divisor * selector)
    gains_total = jnp.sum(gains_sum / divisor[:, None, None], axis=0)
    bias_total = bias_sum / divisor[:, None]
    column_divisor = jnp.concatenate(
        [jnp.full((CLASSES,), divisor[0]), divisor[1:2], jnp.full((3,), divisor[2]), divisor[3:4]]
    )
    out_total = out_sum / column_divisor[None, :]
    row_start = owner_index * shard_rows
    trunk_sum, head_sum = lax.psum((task_grad, head_grad), "dp")
    every_task = lax.all_gather(trunk_sum[None], "task", axis=0, tiled=True)
    scaled, pair_products = mixed_gradient(every_task, divisor)
    mixing = combine_weights(pair_products, conflict)
    combined = jnp.sum(mixing[:, None, None, None, None] * scaled, axis=0)
    head_rows = lax.dynamic_slice_in_dim(head_sum, row_start, shard_rows, 2)
    grad_rows = lax.dynamic_slice_in_dim(combined, row_start, shard_rows, 2)
    grad_cols = lax.dynamic_slice_in_dim(combined, row_start, shard_rows, 3)
    left_new = 0.5 * trunk_left + 0.5 * jnp.einsum(
        "lkio,lkjo->lkij", grad_rows, combined, precision=PRECISE
    )
    right_new = 0.5 * trunk_right + 0.5 * jnp.einsum(
        "lkio,lkip->lkop", grad_cols, combined, precision=PRECISE
    )
    turned = jnp.einsum("lkia,lkaj->lkij", left_root, combined, precision=PRECISE)
    step_rows = jnp.einsum("lkij,lkjo->lkio", turned, right_root, precision=PRECISE)
    master_new = trunk_master - RATE_TRUNK * (step_rows + WEIGHT_DECAY * trunk_master)
    head_one, head_two, head_new = adamw_update(
        head_rows / own_divisor, head_first, head_second, head_master, RATE_MATRIX
    )
    out_one, out_two, out_new = adamw_update(
        out_total, out_first, out_second, out_master, RATE_MATRIX
    )
    gain_one, gain_two, gain_new = adamw_update(
        gains_total, gains_first, gains_second, trunk_gains, RATE_VECTOR
    )
    bias_one, bias_two, bias_new = adamw_update(
        bias_total, bias_first, bias_second, head_bias, RATE_VECTOR
    )
    loss_terms = jnp.concatenate([loss_sum, valid_count[None]])
    return (
        grad_rows,
        left_new,
        right_new,
        master_new,
        master_new.astype(jnp.bfloat16),
        head_one,
        head_two,
        head_new,
        head_new.astype(jnp.bfloat16),
        out_one,
        out_two,
        out_new,
        out_new.astype(jnp.bfloat16),
        gain_one,
        gain_two,
        gain_new,
        bias_one,
        bias_two,
        bias_new,
        loss_terms,
        pair_products,
    )


def solution(mesh):
    placed = (
        P("dp", None, None, None),
        P("dp", None, None),
        P("dp", None, None),
        P("dp", None, None),
        P("dp", None, None, None),
        P("dp"),
        P(),
        P(),
        P(None, None, "dp", None),
        P(None, None, "dp", None),
        P(None, None, "dp", None),
        P(None, None, "dp", None),
        P(None, None, "dp", None),
        P(),
        P("task", None, "dp", None),
        P("task", None, "dp", None),
        P("task", None, "dp", None),
        P("task", None, "dp", None),
        P(),
        P(),
        P(),
        P(),
        P(),
        P(),
        P(),
        P(),
        P(),
        P(),
    )
    return jax.shard_map(
        body,
        mesh=mesh,
        in_specs=placed,
        out_specs=(
            P(None, None, "dp", None),
            P(None, None, "dp", None),
            P(None, None, "dp", None),
            P(None, None, "dp", None),
            P(None, None, "dp", None),
            P("task", None, "dp", None),
            P("task", None, "dp", None),
            P("task", None, "dp", None),
            P("task", None, "dp", None),
            P(),
            P(),
            P(),
            P(),
            P(),
            P(),
            P(),
            P(),
            P(),
            P(),
            P(),
            P(),
        ),
        check_vma=False,
    )
```

profile of v0, /device:TPU:0, one launch (start us, length us, event | category | flops | bytes accessed | tf_op | source)
XLA Modules:
  0.0 2264.9 jit_solution(10663044621236450013)
XLA Ops:
  20.0 37.2 %all_gather.10 = bf16[1,2,512,256]{3,2,1,0:T(8,128)(2,1)} all-gather(bf16[1,2,64,256]{3,2,1,0:T(8,128)(2,1)} %param.42), channel_id=1, replica_groups=mesh['task'=4,'dp'=8] {'dp'}, dimensions={2}, use_global_device_ids=true | all-gather | bytes 589824 | tf_op jit(solution)/shard_map/all_gather | solution.py:191
  57.2 22.4 pad_slice_fusion.16
  79.7 76.1 %all-gather.3.cloned.1.call-done = bf16[2,9,512,512]{3,2,1,0:T(8,128)(2,1)} async-done(((bf16[2,9,64,512]{3,2,1,0:T(8,128)(2,1)}), bf16[2,9,512,512]{3,2,1,0:T(8,128)(2,1)}) %all-gather.3.cloned.1.call-update) | async-done | bytes 9437200 | tf_op jit(solution)/shard_map/all_gather | solution.py:190
  196.6 18.9 fusion.37
  215.4 21.2 fusion.93
  236.6 18.4 all-reduce.13
  259.3 15.8 pad_slice_fusion.8
  322.9 21.2 fusion.92
  344.2 17.8 all-reduce.12
  392.4 18.4 all-reduce.11
  421.1 16.5 pad_slice_fusion
  486.8 26.0 %fusion.90 = (f32[512]{0:T(512)S(1)}, f32[512]{0:T(512)S(1)}, f32[3456,512]{1,0:T(8,128)}) fusion(f32[512]{0:T(512)S(1)} %get-tuple-element.116, f32[3456,512]{1,0:T(8,128)} %get-tuple-element.125, f32[512]{0:T(512)S(1)} %get-tuple-element.119, f32[512]{0:T(512)S(1)} %bitcast.394, f32[512]{0:T(512)S(1)} %bitcast.389, bf16[3456,512]{1,0:T(8,128)(2,1)} %bitcast.382, ...), kind=kOutput, calls=%fused_computation.267 | convolution fusion | flops 1852636160 | bytes 74854400 | tf_op jit(solution)/shard_map/dot_general | solution.py:54
  512.8 18.7 all-reduce.10
  584.8 11.3 maximum_bitcast_fusion
  596.1 597.1 %all-reduce.17.cloned.1.call-done = (f32[1,2,9,512,512]{4,3,2,1,0:T(8,128)}, f32[1,2,512,256]{3,2,1,0:T(8,128)}) async-done(((f32[1,2,9,512,512]{4,3,2,1,0:T(8,128)}, f32[1,2,512,256]{3,2,1,0:T(8,128)}), (f32[1,2,9,512,512]{4,3,2,1,0:T(8,128)}, f32[1,2,512,256]{3,2,1,0:T(8,128)})) %all-reduce.17.cloned.1.call-update) | async-done | bytes 19922960 | tf_op jit(solution)/shard_map/psum | solution.py:287
  1199.7 40.3 %all-reduce.9 = (f32[256,18]{0,1:T(8,128)S(1)}, f32[4,4,512]{2,1,0:T(4,128)S(1)}, f32[4,256]{1,0:T(4,128)S(1)}, f32[4]{0:T(128)S(1)}) all-reduce(f32[256,18]{0,1:T(8,128)S(1)} %fusion.89, f32[4,4,512]{2,1,0:T(4,128)S(1)} %broadcast_multiply_fusion, ...), channel_id=1, replica_groups=mesh['task'=4,'dp'=8] {'task','dp'}, use_global_device_ids=true, to_apply=%region_32.33 | all-reduce | flops 13828 | bytes 110624 | tf_op jit(solution)/shard_map/psum | solution.py:275
  1247.9 388.3 %all-gather.5.cloned.1.call-done = f32[4,2,9,512,512]{4,3,2,1,0:T(8,128)} async-done(((f32[1,2,9,512,512]{4,3,2,1,0:T(8,128)}), f32[4,2,9,512,512]{4,3,2,1,0:T(8,128)}) %all-gather.5.cloned.1.call-update) | async-done | bytes 75497488 | tf_op jit(solution)/shard_map/all_gather | solution.py:288
  1636.2 49.0 %broadcast_divide_fusion = f32[4,2,9,512,512]{4,3,2,1,0:T(8,128)} fusion(f32[4,2,9,512,512]{4,3,2,1,0:T(8,128)} %all-gather.5.cloned.1.call-done, f32[4]{0:T(128)S(1)} %get-tuple-element.69), kind=kLoop, calls=%fused_computation.4 | loop fusion | flops 18874368 | bytes 150994960 | tf_op jit(solution)/shard_map/div | solution.py:149
  1685.1 449.4 %fusion.31 = f32[4,4]{1,0:T(4,128)S(1)} fusion(f32[4,2,9,512,512]{4,3,2,1,0:T(8,128)} %broadcast_divide_fusion), kind=kOutput, calls=%fused_computation.108 | convolution fusion | flops 905969664 | bytes 75497536 | tf_op jit(solution)/shard_map/dot_general | solution.py:151
  2135.3 31.7 %multiply_reduce_fusion = f32[2,9,512,512]{3,2,1,0:T(8,128)S(1)} fusion(f32[4]{0:T(128)S(1)} %broadcast_subtract_fusion, f32[4,2,9,512,512]{4,3,2,1,0:T(8,128)} %all-gather.5.cloned.1.call-done, f32[4]{0:T(128)S(1)} %get-tuple-element.69), kind=kLoop, calls=%fused_computation.3 | loop fusion | flops 51904512 | bytes 94371872 | tf_op jit(solution)/shard_map/reduce_sum | solution.py:291
  2175.1 15.4 fusion.104
  2190.5 26.0 %add_multiply_fusion = f32[2,9,64,512]{3,2,1,0:T(8,128)} fusion(f32[2,9,64,512]{3,2,1,0:T(8,128)S(1)} %copy-done.45, f32[2,9,512,512]{3,2,1,0:T(8,128)} %copy-done.1, s32[]{:T(128)S(6)} %select_n.38), kind=kOutput, calls=%fused_computation.67 | convolution fusion | flops 3625058304 | bytes 28311556 | tf_op jit(solution)/shard_map/lkio,lkip->lkop/dot_general | solution.py:298
  2216.5 24.8 %add_multiply_fusion.1 = f32[2,9,64,512]{3,2,1,0:T(8,128)} fusion(f32[2,9,64,512]{3,2,1,0:T(8,128)} %param.38, f32[2,9,64,512]{3,2,1,0:T(8,128)S(1)} %copy-done.43, f32[2,9,512,512]{3,2,1,0:T(8,128)} %copy-done.1), kind=kOutput, calls=%fused_computation.68 | convolution fusion | flops 3625058304 | bytes 25952256 | tf_op jit(solution)/shard_map/lkio,lkjo->lkij/dot_general | solution.py:295
  2241.4 16.8 fusion.102
  (318 shorter events, 270.9 us)
Async XLA Ops:
  7.2 2167.9 %copy-start = (f32[2,9,64,512]{3,2,1,0:T(8,128)S(1)}, f32[2,9,64,512]{3,2,1,0:T(8,128)}, u32[]{:S(2)}) copy-start(f32[2,9,64,512]{3,2,1,0:T(8,128)} %param.40) | copy-start | bytes 7077892
  7.2 148.6 %all-gather.3.cloned.1.call-start = ((), (), s32[]{:S(2)}) async-start(), calls=%async_computation | async-start | bytes 10616832 | tf_op jit(solution)/shard_map/all_gather | solution.py:190
  7.9 1185.3 %all-reduce.17.cloned.1.call-start = ((), (), s32[]{:S(2)}) async-start(), calls=%async_computation.2 | async-start | bytes 39845888 | tf_op jit(solution)/shard_map/psum | solution.py:287
  275.1 29.5 %copy-start.31 = (bf16[2,36,48,512]{3,2,1,0:T(8,128)(2,1)}, bf16[2,36,48,512]{3,2,1,0:T(8,128)(2,1)S(1)}, u32[]{:S(2)}) copy-start(bf16[2,36,48,512]{3,2,1,0:T(8,128)(2,1)S(1)} %get-tuple-element.87) | copy-start | bytes 10616836
  275.1 35.5 %copy-start.29 = (bf16[2,36,48,512]{3,2,1,0:T(8,128)(2,1)}, bf16[2,36,48,512]{3,2,1,0:T(8,128)(2,1)S(1)}, u32[]{:S(2)}) copy-start(bf16[2,36,48,512]{3,2,1,0:T(8,128)(2,1)S(1)} %get-tuple-element.88) | copy-start | bytes 10616836
  275.1 41.4 %copy-start.27 = (bf16[2,36,48,512]{3,2,1,0:T(8,128)(2,1)}, bf16[2,36,48,512]{3,2,1,0:T(8,128)(2,1)S(1)}, u32[]{:S(2)}) copy-start(bf16[2,36,48,512]{3,2,1,0:T(8,128)(2,1)S(1)} %get-tuple-element.89) | copy-start | bytes 10616836
  418.0 19.6 copy-start.6
  596.1 1040.1 %all-gather.5.cloned.1.call-start = ((), (), s32[]{:S(2)}) async-start(), calls=%async_computation.1 | async-start | bytes 94371840 | tf_op jit(solution)/shard_map/all_gather | solution.py:288
  1193.3 50.0 %copy-start.75 = (f32[4,256]{1,0:T(4,128)S(1)}, f32[4,256]{1,0:T(4,128)}, u32[]{:S(2)}) copy-start(f32[4,256]{1,0:T(4,128)} %param.53) | copy-start | bytes 12292
  1193.3 50.0 %copy-start.83 = (f32[4,256]{1,0:T(4,128)S(1)}, f32[4,256]{1,0:T(4,128)}, u32[]{:S(2)}) copy-start(f32[4,256]{1,0:T(4,128)} %param.55) | copy-start | bytes 12292
  1193.4 50.0 %copy-start.84 = (f32[4,256]{1,0:T(4,128)S(1)}, f32[4,256]{1,0:T(4,128)}, u32[]{:S(2)}) copy-start(f32[4,256]{1,0:T(4,128)} %param.54) | copy-start | bytes 12292
  1193.4 50.7 %copy-start.69 = (f32[4,512]{1,0:T(4,128)S(1)}, f32[4,512]{1,0:T(4,128)}, u32[]{:S(2)}) copy-start(f32[4,512]{1,0:T(4,128)} %param.50) | copy-start | bytes 24580
  1193.4 50.7 %copy-start.76 = (f32[4,512]{1,0:T(4,128)S(1)}, f32[4,512]{1,0:T(4,128)}, u32[]{:S(2)}) copy-start(f32[4,512]{1,0:T(4,128)} %param.52) | copy-start | bytes 24580
  1193.4 50.7 %copy-start.77 = (f32[4,512]{1,0:T(4,128)S(1)}, f32[4,512]{1,0:T(4,128)}, u32[]{:S(2)}) copy-start(f32[4,512]{1,0:T(4,128)} %param.51) | copy-start | bytes 24580
  1193.4 51.3 %copy-start.70 = (f32[256,18]{0,1:T(8,128)S(1)}, f32[256,18]{0,1:T(8,128)}, u32[]{:S(2)}) copy-start(f32[256,18]{0,1:T(8,128)} %param.47) | copy-start | bytes 55300
  1193.4 51.3 %copy-start.71 = (f32[256,18]{0,1:T(8,128)S(1)}, f32[256,18]{0,1:T(8,128)}, u32[]{:S(2)}) copy-start(f32[256,18]{0,1:T(8,128)} %param.49) | copy-start | bytes 55300
  1193.4 51.3 %copy-start.72 = (f32[256,18]{0,1:T(8,128)S(1)}, f32[256,18]{0,1:T(8,128)}, u32[]{:S(2)}) copy-start(f32[256,18]{0,1:T(8,128)} %param.48) | copy-start | bytes 55300
  1193.4 52.0 %copy-start.57 = (f32[1,2,64,256]{3,2,1,0:T(8,128)S(1)}, f32[1,2,64,256]{3,2,1,0:T(8,128)}, u32[]{:S(2)}) copy-start(f32[1,2,64,256]{3,2,1,0:T(8,128)} %param.43) | copy-start | bytes 393220
  1193.5 52.0 %copy-start.58 = (f32[1,2,64,256]{3,2,1,0:T(8,128)S(1)}, f32[1,2,64,256]{3,2,1,0:T(8,128)}, u32[]{:S(2)}) copy-start(f32[1,2,64,256]{3,2,1,0:T(8,128)} %param.45) | copy-start | bytes 393220
  1193.5 52.0 %copy-start.59 = (f32[1,2,64,256]{3,2,1,0:T(8,128)S(1)}, f32[1,2,64,256]{3,2,1,0:T(8,128)}, u32[]{:S(2)}) copy-start(f32[1,2,64,256]{3,2,1,0:T(8,128)} %param.44) | copy-start | bytes 393220
  1685.1 450.1 %copy-start.85 = (s32[4,4]{1,0:T(4,128)S(1)}, s32[4,4]{1,0:T(4,128)}, u32[]{:S(2)}) copy-start(s32[4,4]{1,0:T(4,128)} %param.35) | copy-start | bytes 196
  2134.6 32.4 %copy-start.2 = (f32[4,4]{1,0:T(4,128)}, f32[4,4]{1,0:T(4,128)S(1)}, u32[]{:S(2)}) copy-start(f32[4,4]{1,0:T(4,128)S(1)} %fusion.31) | copy-start | bytes 196
  2190.5 26.0 %copy-start.43 = (f32[2,9,64,512]{3,2,1,0:T(8,128)S(1)}, f32[2,9,64,512]{3,2,1,0:T(8,128)}, u32[]{:S(2)}) copy-start(f32[2,9,64,512]{3,2,1,0:T(8,128)} %constant_dynamic-slice_fusion) | copy-start | bytes 7077892
  2216.5 24.8 %copy-start.46 = (f32[2,9,64,512]{3,2,1,0:T(8,128)S(1)}, f32[2,9,64,512]{3,2,1,0:T(8,128)}, u32[]{:S(2)}) copy-start(f32[2,9,64,512]{3,2,1,0:T(8,128)} %param.37) | copy-start | bytes 7077892
  (70 other events, 316.3 us)
Sparse Core Ops, SparseCore 0:
  10.2 145.4 all-gather.2
  596.2 596.9 all-reduce.16
  1194.8 441.3 all-gather.4
where the time goes:
time: 2270 us; the launch traced here: 2260 us
  waiting for transfers between devices  1060 us (47%)
  matrix products  814 us (36%)
  blocking collectives  151 us (7%)
  other arithmetic  150 us (7%)
  local copies, waits for them, and re-layouts  73.4 us (3%)
    psum x1, waiting for transfers between devices, body(): trunk_sum, head_sum = lax.psum((task_grad, head_grad), 'dp')  597 us
    dot_general x1, matrix products, mixed_gradient(): return (scaled, jnp.dot(flattened, flattened.T, precision=PRECISE))  449 us
    all_gather x1, waiting for transfers between devices, body(): every_task = lax.all_gather(trunk_sum[None], 'task', axis=0, tiled=True)  388 us
    dot_general x27, matrix products, conv_taps(): lax.dot_general(shifted_window, weights[tap_index], contract, preferred_e...  223 us
    all_gather x1, waiting for transfers between devices, body(): lax.all_gather(trunk_copy, 'dp', axis=2, tiled=True)  76.1 us
    slice x3, local copies, waits for them, and re-layouts, tap_pieces(): padded_input[:, DILATION_STEP * kernel_row:DILATION_STEP * kernel_row + f...  54.7 us
    div x1, other arithmetic, mixed_gradient(): scaled = every_task / divisor[:, None, None, None, None]  49 us
    dot_general x18, matrix products, conv_weight_grad(): lax.dot_general(shifted_window, delta_rows, CONTRACT_ROWS, preferred_elem...  47.9 us
  transfers between devices with their start and end apart: 3, of which 3 were waited for; matrix products, arithmetic and copies ran while one was open for 2% of the time, Pallas kernels for 0%

commit v1 on v0

v1 whole, which is shorter than its diff:
```python
import functools

import jax
import jax.numpy as jnp
from jax import lax
from jax.experimental import pallas as pl
from jax.experimental.pallas import tpu as pltpu
from jax.sharding import PartitionSpec as P

BRANCH_WIDTH = 256
CLASSES = 13
TASKS = 4
DILATION_STEP = 2
STEP = 5


PRECISE = lax.Precision.HIGHEST
NORM_EPS = 1e-05
RATE_TRUNK = 0.3
RATE_MATRIX = 0.05
RATE_VECTOR = 0.3
WEIGHT_DECAY = 0.01
ADAM_EPS = 1e-08
GRAM_EPS = 1e-12
PLAIN = (((1,), (0,)), ((), ()))
CONTRACT_ROWS = (((0,), (0,)), ((), ()))
CONTRACT_COLS = (((1,), (1,)), ((), ()))
CHUNK = 9
TILE = 12
PARAMS = pltpu.CompilerParams(vmem_limit_bytes=58 * 1024 * 1024)


def silu_slope(tap_values):
    sigmoid = jax.nn.sigmoid(tap_values)
    return sigmoid * (1.0 + tap_values * (1.0 - sigmoid))


def dot(a, b, contract=PLAIN):
    return lax.dot_general(a, b, contract, preferred_element_type=jnp.float32)


def clear_edges(wide):
    rows = wide.shape[1]
    edge = jnp.zeros((wide.shape[0], DILATION_STEP) + wide.shape[2:], wide.dtype)
    wide[:, 0:DILATION_STEP] = edge
    wide[:, rows - DILATION_STEP : rows] = edge


def spread_columns(wide, image, row, values):
    width, channels = values.shape[1:]
    column = lax.broadcasted_iota(jnp.int32, (1, width, channels), 1)
    left = jnp.where(column >= DILATION_STEP, pltpu.roll(values, DILATION_STEP, 1), 0.0)
    right = jnp.where(
        column < width - DILATION_STEP, pltpu.roll(values, width - DILATION_STEP, 1), 0.0
    )
    place = pl.ds(DILATION_STEP + row, values.shape[0])
    for part, piece in enumerate((left, values, right)):
        wide[image, place, :, part * channels : (part + 1) * channels] = piece.astype(wide.dtype)


def window(wide, image, row, rows, kernel_row, part=None):
    channels = wide.shape[3] // 3
    place = pl.ds(row + DILATION_STEP * kernel_row, rows)
    if part is None:
        return wide[image, place].reshape(rows * wide.shape[2], 3 * channels)
    return wide[image, place, :, part * channels : (part + 1) * channels].reshape(
        rows * wide.shape[2], channels
    )


def conv_tile(wide, weights, image, row, rows):
    channels = weights.shape[1]
    taps = jnp.concatenate([window(wide, image, row, rows, k) for k in range(3)], axis=1)
    return dot(taps, weights[...].reshape(9 * channels, channels))


def conv_tile_back(wide, weights, image, row, rows):
    total = None
    for tap in range(9):
        kernel_row, kernel_column = divmod(tap, 3)
        part = dot(
            window(wide, image, row, rows, 2 - kernel_row, 2 - kernel_column),
            weights[tap],
            CONTRACT_COLS,
        )
        total = part if total is None else total + part
    return total


def add_sums(sums, first, second):
    sums[0:1] += jnp.sum(first, axis=0, keepdims=True)
    sums[1:2] += jnp.sum(second, axis=0, keepdims=True)


def first_kernel(steps, tiles, x_ref, w_ref, conv_ref, sums, wide):
    g = pl.program_id(0)

    @pl.when(g == 0)
    def _():
        clear_edges(wide)
        sums[...] = jnp.zeros_like(sums)

    @pl.when(g < steps)
    def _():
        per = steps // wide.shape[0]

        def one(i, carry):
            spread_columns(
                wide,
                g // per,
                lax.rem(g, per) * CHUNK + 3 * i,
                x_ref[0, pl.ds(3 * i, 3)].astype(jnp.float32),
            )
            return carry

        lax.fori_loop(0, CHUNK // 3, one, 0)
        sums[2:3] += jnp.sum(x_ref[0].astype(jnp.float32), axis=(0, 1))[None]

    @pl.when(g >= steps)
    def _():
        per = tiles // wide.shape[0]
        t = g - steps
        conv = conv_tile(wide, w_ref, t // per, lax.rem(t, per) * TILE, TILE)
        conv_ref[...] = conv
        add_sums(sums, conv, conv * conv)


def second_kernel(steps, tiles, y_ref, v_ref, w_ref, conv_ref, act_ref, sums, wide):
    g = pl.program_id(0)

    @pl.when(g == 0)
    def _():
        clear_edges(wide)
        sums[...] = jnp.zeros_like(sums)

    @pl.when(g < steps)
    def _():
        per = steps // wide.shape[0]

        def one(i, carry):
            values = y_ref[0, pl.ds(3 * i, 3)]
            normed = v_ref[2:3] * ((values - v_ref[0:1]) * v_ref[1:2]) + v_ref[3:4]
            act = jax.nn.silu(normed).astype(jnp.bfloat16)
            act_ref[0, pl.ds(3 * i, 3)] = act
            act = act.astype(jnp.float32)
            spread_columns(wide, g // per, lax.rem(g, per) * CHUNK + 3 * i, act)
            sums[2:3] += jnp.sum(act, axis=(0, 1))[None]
            return carry

        lax.fori_loop(0, CHUNK // 3, one, 0)

    @pl.when(g >= steps)
    def _():
        per = tiles // wide.shape[0]
        t = g - steps
        conv = conv_tile(wide, w_ref, t // per, lax.rem(t, per) * TILE, TILE)
        conv_ref[...] = conv
        add_sums(sums, conv, conv * conv)


def map_specs(images, height, width, channels):
    per = height // CHUNK
    steps = images * per
    stream = pl.BlockSpec(
        (1, CHUNK, width, channels),
        lambda g: (jnp.minimum(g, steps - 1) // per, lax.rem(jnp.minimum(g, steps - 1), per), 0, 0),
    )
    rows = pl.BlockSpec((TILE * width, channels), lambda g: (jnp.maximum(g - steps, 0), 0))
    return steps, images * (height // TILE), stream, rows


def fixed(*shape):
    return pl.BlockSpec(shape, lambda g: (0,) * len(shape))


def first_conv_call(x, weights):
    images, height, width, channels = x.shape
    steps, tiles, stream, rows = map_specs(*x.shape)
    pixels = images * height * width
    return pl.pallas_call(
        functools.partial(first_kernel, steps, tiles),
        grid=(steps + tiles,),
        in_specs=[stream, fixed(*weights.shape)],
        out_specs=(rows, fixed(8, channels)),
        out_shape=(
            jax.ShapeDtypeStruct((pixels, channels), jnp.float32),
            jax.ShapeDtypeStruct((8, channels), jnp.float32),
        ),
        scratch_shapes=[
            pltpu.VMEM((images, height + 2 * DILATION_STEP, width, 3 * channels), jnp.bfloat16)
        ],
        compiler_params=PARAMS,
        name="first_conv",
    )(x, weights)


def second_conv_call(y, vectors, weights, shape):
    images, height, width, channels = shape
    steps, tiles, stream, rows = map_specs(*shape)
    pixels = images * height * width
    return pl.pallas_call(
        functools.partial(second_kernel, steps, tiles),
        grid=(steps + tiles,),
        in_specs=[stream, fixed(8, channels), fixed(*weights.shape)],
        out_specs=(rows, stream, fixed(8, channels)),
        out_shape=(
            jax.ShapeDtypeStruct((pixels, channels), jnp.float32),
            jax.ShapeDtypeStruct(shape, jnp.bfloat16),
            jax.ShapeDtypeStruct((8, channels), jnp.float32),
        ),
        scratch_shapes=[
            pltpu.VMEM((images, height + 2 * DILATION_STEP, width, 3 * channels), jnp.bfloat16)
        ],
        compiler_params=PARAMS,
        name="second_conv",
    )(y.reshape(shape), vectors, weights)


def weight_kernel(steps, keep_back, x_ref, up_ref, y_ref, v_ref, mean_ref, grad_ref, edge_ref, *rest):
    wide, back = rest[-2:]
    g = pl.program_id(0)
    images, padded, width, channels = wide.shape
    channels = channels // 3
    height = padded - 2 * DILATION_STEP

    @pl.when(g == 0)
    def _():
        clear_edges(wide)
        edge_ref[...] = jnp.zeros_like(edge_ref)

    @pl.when(g < steps)
    def _():
        per = steps // images
        column = lax.broadcasted_iota(jnp.int32, (1, width, channels), 1)

        def one(i, carry):
            place = pl.ds(3 * i, 3)
            row = lax.rem(g, per) * CHUNK + 3 * i
            spread_columns(wide, g // per, row, x_ref[0, place].astype(jnp.float32))
            centered = (y_ref[0, place] - v_ref[0:1]) * v_ref[1:2]
            values = v_ref[2:3] * v_ref[1:2] * (
                up_ref[0, place] - v_ref[4:5] - centered * v_ref[5:6]
            )
            values = values.astype(jnp.bfloat16)
            if keep_back:
                rest[0][0, place] = values
            back[g // per, pl.ds(row, 3)] = values
            values = values.astype(jnp.float32)
            for kernel_column in range(3):
                shift = DILATION_STEP * (kernel_column - 1)
                inside = (column + shift >= 0) & (column + shift < width)
                line = jnp.sum(jnp.where(inside, values, 0.0), axis=1)
                for kernel_row in range(3):
                    at = row + DILATION_STEP * (kernel_row - 1)
                    part = [
                        jnp.where((at + r >= 0) & (at + r < height), line[r : r + 1], 0.0)
                        for r in range(3)
                    ]
                    tap = 3 * kernel_row + kernel_column
                    edge_ref[tap : tap + 1] += part[0] + part[1] + part[2]
            return carry

        lax.fori_loop(0, CHUNK // 3, one, 0)

    for column in range(3):

        @pl.when((g >= steps) & (lax.rem(g - steps, 3) == column))
        def _():
            total = None
            for image in range(images):
                part = dot(
                    window(wide, image, 0, height, (g - steps) // 3, column),
                    back[image].reshape(height * width, channels),
                    CONTRACT_ROWS,
                )
                total = part if total is None else total + part
            line = edge_ref[pl.ds(g - steps, 1)]
            grad_ref[0] = (total - mean_ref[...] * line).astype(grad_ref.dtype)


def weight_grad_call(x, upstream, y, vectors, mean, keep_back):
    images, height, width, channels = x.shape
    steps, tiles, stream, rows = map_specs(*x.shape)
    out_specs = [
        pl.BlockSpec((1, channels, channels), lambda g: (jnp.maximum(g - steps, 0), 0, 0)),
        fixed(16, channels),
    ]
    out_shape = [
        jax.ShapeDtypeStruct((9, channels, channels), jnp.bfloat16),
        jax.ShapeDtypeStruct((16, channels), jnp.float32),
    ]
    if keep_back:
        out_specs.append(stream)
        out_shape.append(jax.ShapeDtypeStruct(x.shape, jnp.bfloat16))
    return pl.pallas_call(
        functools.partial(weight_kernel, steps, keep_back),
        grid=(steps + 9,),
        in_specs=[stream, stream, stream, fixed(8, channels), fixed(channels, 1)],
        out_specs=tuple(out_specs),
        out_shape=tuple(out_shape),
        scratch_shapes=[
            pltpu.VMEM((images, height + 2 * DILATION_STEP, width, 3 * channels), jnp.bfloat16),
            pltpu.VMEM((images, height, width, channels), jnp.bfloat16),
        ],
        compiler_params=PARAMS,
        name="weight_grad",
    )(x, upstream.reshape(x.shape), y.reshape(x.shape), vectors, mean.reshape(channels, 1))


def act_grad_kernel(steps, tiles, back_ref, y_ref, v_ref, w_ref, up_ref, sums, wide):
    g = pl.program_id(0)

    @pl.when(g == 0)
    def _():
        clear_edges(wide)
        sums[...] = jnp.zeros_like(sums)

    @pl.when(g < steps)
    def _():
        per = steps // wide.shape[0]

        def one(i, carry):
            spread_columns(
                wide,
                g // per,
                lax.rem(g, per) * CHUNK + 3 * i,
                back_ref[0, pl.ds(3 * i, 3)].astype(jnp.float32),
            )
            return carry

        lax.fori_loop(0, CHUNK // 3, one, 0)

    @pl.when(g >= steps)
    def _():
        per = tiles // wide.shape[0]
        t = g - steps
        grad = conv_tile_back(wide, w_ref, t // per, lax.rem(t, per) * TILE, TILE)
        centered = (y_ref[...] - v_ref[0:1]) * v_ref[1:2]
        upstream = grad * silu_slope(v_ref[2:3] * centered + v_ref[3:4])
        up_ref[...] = upstream
        add_sums(sums, upstream, upstream * centered)


def act_grad_call(back, y, vectors, weights):
    images, height, width, channels = back.shape
    steps, tiles, stream, rows = map_specs(*back.shape)
    pixels = images * height * width
    return pl.pallas_call(
        functools.partial(act_grad_kernel, steps, tiles),
        grid=(steps + tiles,),
        in_specs=[stream, rows, fixed(8, channels), fixed(*weights.shape)],
        out_specs=(rows, fixed(8, channels)),
        out_shape=(
            jax.ShapeDtypeStruct((pixels, channels), jnp.float32),
            jax.ShapeDtypeStruct((8, channels), jnp.float32),
        ),
        scratch_shapes=[
            pltpu.VMEM((images, height + 2 * DILATION_STEP, width, 3 * channels), jnp.bfloat16)
        ],
        compiler_params=PARAMS,
        name="act_grad",
    )(back, y, vectors, weights)


def update_kernel(
    g_ref, rows_ref, cols_ref, left_ref, right_ref, master_ref, lroot_ref,
    rroot_ref, grad_out, left_out, right_out, master_out, copy_out,
):
    full = g_ref[0]
    rows = rows_ref[0]
    grad_out[0] = rows.astype(jnp.float32)
    left_out[0] = 0.5 * left_ref[0] + 0.5 * dot(rows, full, CONTRACT_COLS)
    right_out[0] = 0.5 * right_ref[0] + 0.5 * dot(cols_ref[0], full)
    turned = dot(lroot_ref[0].astype(jnp.bfloat16), full).astype(jnp.bfloat16)
    step = dot(turned, rroot_ref[0].astype(jnp.bfloat16))
    master = master_ref[0]
    master = master - RATE_TRUNK * (step + WEIGHT_DECAY * master)
    master_out[0] = master
    copy_out[0] = master.astype(jnp.bfloat16)


def update_call(owner, combined, left, right, master, lroot, rroot):
    layers, taps, shard_rows, channels = left.shape
    count = layers * taps
    one = pl.BlockSpec((1, shard_rows, channels), lambda g: (g, 0, 0))
    whole = pl.BlockSpec((1, channels, channels), lambda g: (g, 0, 0))
    flat = (count, shard_rows, channels)
    start = owner * shard_rows
    rows = lax.dynamic_slice_in_dim(combined, start, shard_rows, 1)
    cols = jnp.swapaxes(lax.dynamic_slice_in_dim(combined, start, shard_rows, 2), 1, 2)
    outs = pl.pallas_call(
        update_kernel,
        grid=(count,),
        in_specs=[whole, one, one, one, one, one, one, whole],
        out_specs=(one,) * 5,
        out_shape=tuple(
            jax.ShapeDtypeStruct(flat, kind)
            for kind in (jnp.float32, jnp.float32, jnp.float32, jnp.float32, jnp.bfloat16)
        ),
        compiler_params=PARAMS,
        name="update",
    )(
        combined,
        rows,
        cols,
        left.reshape(flat),
        right.reshape(flat),
        master.reshape(flat),
        lroot.reshape(flat),
        rroot.reshape(count, channels, channels),
    )
    return [out.reshape(left.shape) for out in outs]


def small_sum_kernel(members, x_ref, out_ref, slots, send_sem, recv_sem):
    me = lax.axis_index("dp")
    barrier = pltpu.get_barrier_semaphore()
    for k in range(1, members):
        pl.semaphore_signal(
            barrier,
            inc=1,
            device_id={"dp": lax.rem(me + k, members)},
            device_id_type=pl.DeviceIdType.MESH,
        )
    pl.semaphore_wait(barrier, members - 1)
    copies = []
    for k in range(1, members):
        copy = pltpu.make_async_remote_copy(
            src_ref=x_ref,
            dst_ref=slots.at[me],
            send_sem=send_sem.at[k],
            recv_sem=recv_sem.at[me],
            device_id={"dp": lax.rem(me + k, members)},
            device_id_type=pl.DeviceIdType.MESH,
        )
        copy.start()
        copies.append(copy)
    slots[me] = x_ref[...]
    for k in range(1, members):
        source = lax.rem(me + k, members)
        pltpu.make_async_remote_copy(
            src_ref=x_ref,
            dst_ref=slots.at[source],
            send_sem=send_sem.at[k],
            recv_sem=recv_sem.at[source],
            device_id={"dp": source},
            device_id_type=pl.DeviceIdType.MESH,
        ).wait_recv()
    total = slots[0]
    for k in range(1, members):
        total = total + slots[k]
    out_ref[...] = total
    for copy in copies:
        copy.wait_send()


def small_sum(x, identity):
    members = lax.axis_size("dp")
    return pl.pallas_call(
        functools.partial(small_sum_kernel, members),
        out_shape=jax.ShapeDtypeStruct(x.shape, jnp.float32),
        in_specs=[pl.BlockSpec(memory_space=pltpu.VMEM)],
        out_specs=pl.BlockSpec(memory_space=pltpu.VMEM),
        scratch_shapes=[
            pltpu.VMEM((members,) + x.shape, jnp.float32),
            pltpu.SemaphoreType.DMA((members,)),
            pltpu.SemaphoreType.DMA((members,)),
        ],
        compiler_params=pltpu.CompilerParams(collective_id=identity, has_side_effects=True),
        name="small_sum",
    )(x)


def scatter_sum(parts):
    members = lax.axis_size("dp")
    me = lax.axis_index("dp")
    taps, channels, width = parts.shape
    held = parts.reshape(taps, members, channels // members, width)
    bit = 1
    while bit < members:
        held = held.reshape(taps, -1, 2, channels // members, width)
        mine = lax.rem(me // bit, 2)
        other = lax.dynamic_index_in_dim(held, 1 - mine, 2, keepdims=False)
        keep = lax.dynamic_index_in_dim(held, mine, 2, keepdims=False)
        other = lax.ppermute(
            other.astype(jnp.bfloat16), "dp", [(i, i ^ bit) for i in range(members)]
        )
        held = keep.astype(jnp.float32) + other.astype(jnp.float32)
        bit *= 2
    return held.reshape(taps, channels // members, width)


def pad_rows(parts, rows):
    used = sum(part.shape[0] for part in parts)
    if used < rows:
        parts = list(parts) + [jnp.zeros((rows - used, parts[0].shape[1]), jnp.float32)]
    return jnp.concatenate(parts)


def norm_vectors(totals, gain, shift, pixels):
    center = totals[0] / pixels
    inverse = lax.rsqrt(totals[1] / pixels - center * center + NORM_EPS)
    return center, inverse, gain, shift


def stack_vectors(parts):
    zero = jnp.zeros_like(parts[0])
    return jnp.stack(list(parts) + [zero] * (8 - len(parts)))


def boundary(labels):
    across = jnp.pad(
        (labels[:, :, 1:] != labels[:, :, :-1]).astype(jnp.float32), ((0, 0), (0, 0), (0, 1))
    )
    downward = jnp.pad(
        (labels[:, 1:, :] != labels[:, :-1, :]).astype(jnp.float32), ((0, 0), (0, 1), (0, 0))
    )
    return jnp.maximum(across, downward)


def pixel_data(labels, depth_mask, depth_target, normal_target, scene_ids, task_weights):
    images, feature_rows, feature_columns = labels.shape
    choose = (scene_ids[:, None] == jnp.arange(task_weights.shape[0])[None, :]).astype(jnp.float32)
    per_image = jnp.dot(choose, task_weights, precision=PRECISE)
    return (
        labels.reshape(-1),
        depth_mask.reshape(-1).astype(jnp.float32),
        boundary(labels).reshape(-1),
        depth_target.reshape(-1),
        jnp.transpose(normal_target, (0, 2, 3, 1)).reshape(-1, 3),
        jnp.repeat(per_image, feature_rows * feature_columns, axis=0),
    )


def task_sums(logits, pixel_info):
    labels, valid_mask, edge_target, depth_values, normals, weights = pixel_info
    classes = logits[:, :CLASSES]
    largest = jnp.max(classes, axis=1, keepdims=True)
    spread = jnp.log(jnp.sum(jnp.exp(classes - largest), axis=1)) + largest[:, 0]
    picked = jnp.sum(
        jnp.where(labels[:, None] == jnp.arange(CLASSES)[None, :], classes, 0.0), axis=1
    )
    segment = jnp.sum(weights[:, 0] * (spread - picked))
    offset = logits[:, CLASSES] - depth_values
    distance = jnp.sum(weights[:, 1] * valid_mask * (jnp.sqrt(offset * offset + 1.0) - 1.0))
    predicted = logits[:, CLASSES + 1 : CLASSES + 4]
    cosine = jnp.sum(predicted * normals, axis=1) * lax.rsqrt(
        (jnp.sum(predicted * predicted, axis=1) + 1.0) * (jnp.sum(normals * normals, axis=1) + 1.0)
    )
    surface = jnp.sum(weights[:, 2] * (1.0 - cosine))
    edge_logit = logits[:, CLASSES + 4]
    contour = jnp.sum(weights[:, 3] * (jax.nn.softplus(edge_logit) - edge_target * edge_logit))
    return jnp.stack([segment, distance, surface, contour])


def combine_weights(pair_products, conflict):
    offdiagonal = (1.0 - jnp.eye(TASKS, dtype=jnp.float32)) * conflict.astype(jnp.float32)
    ratios = offdiagonal * pair_products / (jnp.diagonal(pair_products)[None, :] + GRAM_EPS)
    return 1.0 - jnp.sum(ratios, axis=0)


def adamw_update(gradient, moment_one, moment_two, weight, rate):
    moment_one = 0.5 * moment_one + 0.5 * gradient
    moment_two = 0.5 * moment_two + 0.5 * gradient * gradient
    correction = 1.0 - 0.5**STEP
    weight = weight - rate * (
        moment_one / correction / (jnp.sqrt(moment_two / correction) + ADAM_EPS)
        + WEIGHT_DECAY * weight
    )
    return (moment_one, moment_two, weight)


def body(
    features,
    labels,
    depth_mask,
    depth_target,
    normal_target,
    scene_ids,
    task_weights,
    conflict,
    trunk_copy,
    trunk_master,
    trunk_left,
    trunk_right,
    left_root,
    right_root,
    head_copy,
    head_master,
    head_first,
    head_second,
    out_copy,
    out_master,
    out_first,
    out_second,
    trunk_gains,
    gains_first,
    gains_second,
    head_bias,
    bias_first,
    bias_second,
):
    images, feature_rows, feature_columns, channels = features.shape
    pixels = jnp.array(images * feature_rows * feature_columns * lax.axis_size("dp"), jnp.float32)
    task_index = lax.axis_index("task")
    owner_index = lax.axis_index("dp")
    trunk_first = lax.all_gather(trunk_copy[0], "dp", axis=1, tiled=True)
    trunk_second = lax.all_gather(trunk_copy[1], "dp", axis=1, tiled=True)
    head_full = lax.all_gather(head_copy, "dp", axis=2, tiled=True)
    pixel_info = pixel_data(
        labels, depth_mask, depth_target, normal_target, scene_ids, task_weights
    )
    local_valid = jnp.sum(pixel_info[1])
    first_conv, first_sums = first_conv_call(features, trunk_first)
    first_totals = small_sum(
        pad_rows([first_sums[:3], jnp.full((1, channels), local_valid)], 8), 0
    )
    valid_count = first_totals[3, 0]
    first_norm = norm_vectors(first_totals, trunk_gains[0], trunk_gains[1], pixels)
    second_conv, first_act, second_sums = second_conv_call(
        first_conv, stack_vectors(first_norm), trunk_second, features.shape
    )
    second_totals = small_sum(second_sums, 1)
    second_norm = norm_vectors(second_totals, trunk_gains[2], trunk_gains[3], pixels)
    second_center = (second_conv - second_norm[0]) * second_norm[1]
    residual_in = (
        trunk_gains[2] * second_center + trunk_gains[3] + features.reshape(-1, channels)
    )
    trunk_out = jax.nn.silu(residual_in).astype(jnp.bfloat16)
    pooled = jnp.mean(trunk_out.reshape(images, -1, channels), axis=1, dtype=jnp.float32).astype(
        jnp.bfloat16
    )
    selector = (jnp.arange(TASKS) == task_index).astype(jnp.float32)
    own_bias = jnp.dot(selector, head_bias, precision=PRECISE)
    head_pre = jnp.dot(trunk_out, head_full[0, 0], preferred_element_type=jnp.float32).reshape(
        images, -1, BRANCH_WIDTH
    )
    head_pre = (
        head_pre
        + jnp.dot(pooled, head_full[0, 1], preferred_element_type=jnp.float32)[:, None, :]
        + own_bias
    )
    head_pre = head_pre.reshape(-1, BRANCH_WIDTH)
    hidden_act = jax.nn.silu(head_pre).astype(jnp.bfloat16)
    logits = jnp.dot(hidden_act, out_copy, preferred_element_type=jnp.float32)
    totals, pullback = jax.vjp(lambda tap_values: task_sums(tap_values, pixel_info), logits)
    logit_grad = pullback(selector)[0].astype(jnp.bfloat16)
    out_grad = dot(hidden_act, logit_grad, CONTRACT_ROWS)
    hidden_grad = dot(logit_grad, out_copy, CONTRACT_COLS)
    pre_grad = (hidden_grad * silu_slope(head_pre)).astype(jnp.bfloat16)
    bias_grad = jnp.sum(pre_grad, axis=0, dtype=jnp.float32)
    per_image = jnp.sum(pre_grad.reshape(images, -1, BRANCH_WIDTH), axis=1, dtype=jnp.float32)
    input_grad = dot(trunk_out, pre_grad, CONTRACT_ROWS)
    pool_grad = jnp.dot(pooled.astype(jnp.float32).T, per_image, precision=PRECISE)
    pooled_back = jnp.dot(per_image, head_full[0, 1].astype(jnp.float32).T, precision=PRECISE)
    out_back = dot(pre_grad, head_full[0, 0], CONTRACT_COLS)
    out_back = (
        out_back.reshape(images, -1, channels)
        + pooled_back[:, None, :] / (feature_rows * feature_columns)
    ).reshape(-1, channels)
    second_up = out_back * silu_slope(residual_in)
    second_back_sums = small_sum(
        pad_rows(
            [
                jnp.sum(second_up, axis=0, keepdims=True),
                jnp.sum(second_up * second_center, axis=0, keepdims=True),
            ],
            8,
        ),
        2,
    )[:2]
    second_mean = second_totals[2] / pixels
    second_weight, second_edges, second_back = weight_grad_call(
        first_act,
        second_up,
        second_conv,
        stack_vectors(second_norm + tuple(second_back_sums / pixels)),
        second_mean,
        True,
    )
    second_sum = scatter_sum(second_weight)
    first_up, first_up_sums = act_grad_call(
        second_back, first_conv, stack_vectors(first_norm), trunk_second
    )
    first_back_sums = small_sum(first_up_sums, 3)[:2]
    first_mean = first_totals[2] / pixels
    first_weight, first_edges = weight_grad_call(
        features,
        first_up,
        first_conv,
        stack_vectors(first_norm + tuple(first_back_sums / pixels)),
        first_mean,
        False,
    )
    first_sum = scatter_sum(first_weight)
    edges = small_sum(jnp.concatenate([first_edges, second_edges]), 4).reshape(2, 16, 1, channels)
    means = jnp.stack([first_mean, second_mean])
    shard_rows = trunk_copy.shape[2]
    own_means = lax.dynamic_slice_in_dim(means, owner_index * shard_rows, shard_rows, 1)
    removed = (own_means[:, None, :, None] * edges[:, :9]).reshape(18, shard_rows, channels)
    head_grad = jnp.stack([input_grad, pool_grad])[None]
    leading = (owner_index == 0).astype(jnp.float32)
    gains_part = (
        selector[:, None, None]
        * (
            leading
            * jnp.stack(
                [first_back_sums[1], first_back_sums[0], second_back_sums[1], second_back_sums[0]]
            )
        )[None]
    )
    bias_part = selector[:, None] * bias_grad[None]
    loss_part = totals * selector
    gains_sum, bias_sum, out_sum, loss_sum = lax.psum(
        (gains_part, bias_part, out_grad, loss_part), ("task", "dp")
    )
    divisor = jnp.stack([pixels, valid_count, pixels, pixels])
    own_divisor = jnp.sum(divisor * selector)
    gains_total = jnp.sum(gains_sum / divisor[:, None, None], axis=0)
    bias_total = bias_sum / divisor[:, None]
    column_divisor = jnp.concatenate(
        [jnp.full((CLASSES,), divisor[0]), divisor[1:2], jnp.full((3,), divisor[2]), divisor[3:4]]
    )
    out_total = out_sum / column_divisor[None, :]
    head_rows = lax.psum_scatter(head_grad, "dp", scatter_dimension=2, tiled=True)
    own_scaled = (
        (jnp.concatenate([first_sum, second_sum]) + removed) / own_divisor
    ).astype(jnp.bfloat16)
    taps, shard_rows = own_scaled.shape[:2]
    pieces = own_scaled.reshape(taps, shard_rows, TASKS, channels // TASKS)
    scaled = lax.all_to_all(pieces, "task", split_axis=2, concat_axis=0, tiled=False)
    scaled = scaled.reshape(TASKS, taps * shard_rows, channels // TASKS).astype(jnp.float32)
    products = {
        (i, j): jnp.sum(scaled[i] * scaled[j]) for i in range(TASKS) for j in range(i, TASKS)
    }
    pair_products = lax.psum(
        jnp.stack(
            [products[min(i, j), max(i, j)] for i in range(TASKS) for j in range(TASKS)]
        ).reshape(TASKS, TASKS),
        ("task", "dp"),
    )
    mixing = combine_weights(pair_products, conflict)
    quarter = jnp.sum(mixing[:, None, None] * scaled, axis=0).astype(jnp.bfloat16)
    quarter = quarter.reshape(taps, shard_rows, channels // TASKS)
    combined = lax.all_gather(
        lax.all_gather(quarter, "task", axis=2, tiled=True), "dp", axis=1, tiled=True
    )
    grad_rows, left_new, right_new, master_new, copy_new = update_call(
        owner_index, combined, trunk_left, trunk_right, trunk_master, left_root, right_root
    )
    head_one, head_two, head_new = adamw_update(
        head_rows / own_divisor, head_first, head_second, head_master, RATE_MATRIX
    )
    out_one, out_two, out_new = adamw_update(
        out_total, out_first, out_second, out_master, RATE_MATRIX
    )
    gain_one, gain_two, gain_new = adamw_update(
        gains_total, gains_first, gains_second, trunk_gains, RATE_VECTOR
    )
    bias_one, bias_two, bias_new = adamw_update(
        bias_total, bias_first, bias_second, head_bias, RATE_VECTOR
    )
    loss_terms = jnp.concatenate([loss_sum, valid_count[None]])
    return (
        grad_rows,
        left_new,
        right_new,
        master_new,
        copy_new,
        head_one,
        head_two,
        head_new,
        head_new.astype(jnp.bfloat16),
        out_one,
        out_two,
        out_new,
        out_new.astype(jnp.bfloat16),
        gain_one,
        gain_two,
        gain_new,
        bias_one,
        bias_two,
        bias_new,
        loss_terms,
        pair_products,
    )


def solution(mesh):
    rows = P(None, None, "dp", None)
    heads = P("task", None, "dp", None)
    images = P("dp")
    placed = (
        (images,) * 6
        + (P(), P())
        + (rows,) * 5
        + (P(),)
        + (heads,) * 4
        + (P(),) * 10
    )
    return jax.shard_map(
        body,
        mesh=mesh,
        in_specs=placed,
        out_specs=(rows,) * 5 + (heads,) * 4 + (P(),) * 12,
        check_vma=False,
    )
```

time: 2270 us -> 882 us (0.39)
  matrix products: 814 us -> 9.62 us
  waiting for transfers between devices: 1060 us -> 392 us
  Pallas kernels: 0 us -> 248 us
  other arithmetic: 150 us -> 64.1 us
  blocking collectives: 151 us -> 76.1 us
    dot_general x54 -> x4, matrix products: 809 us -> 6.22 us  [dot(): return lax.dot_general(a, b, contract, preferred_element_type=jnp.float32)]
    psum x1 -> x0, waiting for transfers between devices: 597 us -> none  [body(): trunk_sum, head_sum = lax.psum((task_grad, head_grad), 'dp')]
    pallas_call x0 -> x11, Pallas kernels: none -> 248 us  [the longest x5 74.9 us: small_sum(): pl.pallas_call(functools.partial(small_sum_kernel, members), out_shape=ja...]
    all_gather x2 -> x4, waiting for transfers between devices: 464 us -> 232 us  [the longest x1 134 us: body(): lax.all_gather(lax.all_gather(quarter, 'task', axis=2, tiled=True), 'dp',...]
    ppermute x0 -> x6, waiting for transfers between devices: none -> 82.3 us  [scatter_sum(): lax.ppermute(other.astype(jnp.bfloat16), 'dp', [(i, i ^ bit) for i in ran...]
    psum x5 -> x1, blocking collectives: 114 us -> 39.5 us  [body(): lax.psum(jnp.stack([products[min(i, j), max(i, j)] for i in range(TASKS)...]
    reduce_scatter x0 -> x1, waiting for transfers between devices: none -> 66.6 us  [body(): lax.psum_scatter(head_grad, 'dp', scatter_dimension=2, tiled=True)]
    slice x4 -> x6, local copies, waits for them, and re-layouts: 55.6 us -> 6.91 us  [the longest x1 2.42 us: body(): trunk_second = lax.all_gather(trunk_copy[1], 'dp', axis=1, tiled=True)]
  transfers between devices with their start and end apart: 3 -> 12, of which waited for: 3 -> 9; matrix products, arithmetic and copies ran while one was open for 2% -> 6% of each run, Pallas kernels for 0% -> 17%
where the time goes in v1:
time: 882 us; the launch traced here: 874 us
  waiting for transfers between devices  392 us (44%)
  Pallas kernels  248 us (28%)
  blocking collectives  76.1 us (9%)
  other arithmetic  64.1 us (7%)
  local copies, waits for them, and re-layouts  56.6 us (6%)
  between operations  15.5 us (2%)
  starting transfers between devices  11.7 us (1%)
  matrix products  9.62 us (1%)
    all_gather x1, waiting for transfers between devices, body(): lax.all_gather(lax.all_gather(quarter, 'task', axis=2, tiled=True), 'dp',...  134 us
    ppermute x6, waiting for transfers between devices, scatter_sum(): lax.ppermute(other.astype(jnp.bfloat16), 'dp', [(i, i ^ bit) for i in ran...  82.3 us
    pallas_call x5, Pallas kernels, small_sum(): pl.pallas_call(functools.partial(small_sum_kernel, members), out_shape=ja...  74.9 us
    reduce_scatter x1, waiting for transfers between devices, body(): lax.psum_scatter(head_grad, 'dp', scatter_dimension=2, tiled=True)  66.6 us
    pallas_call x2, Pallas kernels, weight_grad_call(): pl.pallas_call(functools.partial(weight_kernel, steps, keep_back), grid=(...  64.8 us
    all_gather x1, waiting for transfers between devices, body(): trunk_second = lax.all_gather(trunk_copy[1], 'dp', axis=1, tiled=True)  43.6 us
    all_gather x1, waiting for transfers between devices, body(): trunk_first = lax.all_gather(trunk_copy[0], 'dp', axis=1, tiled=True)  40.2 us
    psum x1, blocking collectives, body(): lax.psum(jnp.stack([products[min(i, j), max(i, j)] for i in range(TASKS)...  39.5 us
  transfers between devices with their start and end apart: 12, of which 9 were waited for; matrix products, arithmetic and copies ran while one was open for 6% of the time, Pallas kernels for 17%

profile of v1, /device:TPU:0, one launch (start us, length us, event | category | flops | bytes accessed | tf_op | source)
XLA Modules:
  0.0 873.8 jit_solution(12224847370718543218)
XLA Ops:
  20.8 36.6 %all_gather.17 = bf16[1,2,512,256]{3,2,1,0:T(8,128)(2,1)} all-gather(bf16[1,2,64,256]{3,2,1,0:T(8,128)(2,1)S(1)} %copy-done.37), channel_id=1, replica_groups=mesh['task'=4,'dp'=8] {'dp'}, dimensions={2}, use_global_device_ids=true | all-gather | bytes 589824 | tf_op jit(solution)/shard_map/all_gather | solution.py:609
  57.4 40.2 %all-gather.11.cloned.1.call-done = bf16[1,9,512,512]{3,2,1,0:T(8,128)(2,1)} async-done(((bf16[1,9,64,512]{3,2,1,0:T(8,128)(2,1)}), bf16[1,9,512,512]{3,2,1,0:T(8,128)(2,1)}) %all-gather.11.cloned.1.call-update) | async-done | bytes 4718608 | tf_op jit(solution)/shard_map/all_gather | solution.py:607
  97.6 26.3 %first_conv.1 = (f32[3456,512]{1,0:T(8,128)}, f32[8,512]{1,0:T(8,128)}) custom-call(bf16[2,36,48,512]{3,2,1,0:T(8,128)(2,1)} %x_ref.3, bf16[9,512,512]{2,1,0:T(8,128)(2,1)} %bitcast.179), custom_call_target="tpu_custom_call" | custom-call | tf_op jit(solution)/shard_map/first_conv/pallas_call | solution.py:180
  125.3 8.2 small_sum.5
  136.2 43.6 %all-gather.13.cloned.1.call-done = bf16[1,9,512,512]{3,2,1,0:T(8,128)(2,1)} async-done(((bf16[1,9,64,512]{3,2,1,0:T(8,128)(2,1)}), bf16[1,9,512,512]{3,2,1,0:T(8,128)(2,1)}) %all-gather.13.cloned.1.call-update) | async-done | bytes 4718608 | tf_op jit(solution)/shard_map/all_gather | solution.py:608
  179.8 28.8 %second_conv.1 = (f32[3456,512]{1,0:T(8,128)}, bf16[2,36,48,512]{3,2,1,0:T(8,128)(2,1)}, f32[8,512]{1,0:T(8,128)}) custom-call(f32[2,36,48,512]{3,2,1,0:T(8,128)} %bitcast.160, f32[8,512]{1,0:T(8,128)} %maximum_maximum_fusion.1.v_ref, bf16[9,512,512]{2,1,0:T(8,128)(2,1)} %bitcast.171), custom_call_target="tpu_custom_call" | custom-call | tf_op jit(solution)/shard_map/second_conv/pallas_call | solution.py:201
  208.7 7.9 small_sum.6
  241.9 6.9 fusion.44
  249.5 7.9 small_sum.7
  259.4 32.8 %weight_grad.2 = (bf16[9,512,512]{2,1,0:T(8,128)(2,1)}, f32[16,512]{1,0:T(8,128)}, bf16[2,36,48,512]{3,2,1,0:T(8,128)(2,1)}) custom-call(bf16[2,36,48,512]{3,2,1,0:T(8,128)(2,1)} %get-tuple-element.40.x_ref, f32[2,36,48,512]{3,2,1,0:T(8,128)} %bitcast.167, f32[2,36,48,512]{3,2,1,0:T(8,128)} %bitcast.162, f32[8,512]{1,0:T(8,128)} %stack.93.v_ref, ...), custom_call_target="tpu_custom_call" | custom-call | tf_op jit(solution)/shard_map/weight_grad/pallas_call | solution.py:295
  296.0 28.8 %act_grad.1 = (f32[3456,512]{1,0:T(8,128)}, f32[8,512]{1,0:T(8,128)}) custom-call(bf16[2,36,48,512]{3,2,1,0:T(8,128)(2,1)} %get-tuple-element.43.back_ref, f32[3456,512]{1,0:T(8,128)} %get-tuple-element.38.y_ref, f32[8,512]{1,0:T(8,128)} %maximum_maximum_fusion.1.v_ref, bf16[9,512,512]{2,1,0:T(8,128)(2,1)} %bitcast.172), custom_call_target="tpu_custom_call" | custom-call | tf_op jit(solution)/shard_map/act_grad/pallas_call | solution.py:348
  324.8 22.2 %small_sum.8 = f32[8,512]{1,0:T(8,128)} custom-call(f32[8,512]{1,0:T(8,128)} %get-tuple-element.45.x_ref), custom_call_target="tpu_custom_call" | custom-call | tf_op jit(solution)/shard_map/small_sum/pallas_call | solution.py:459
  348.3 32.0 %weight_grad.3 = (bf16[9,512,512]{2,1,0:T(8,128)(2,1)}, f32[16,512]{1,0:T(8,128)}) custom-call(bf16[2,36,48,512]{3,2,1,0:T(8,128)(2,1)} %x_ref.3, f32[2,36,48,512]{3,2,1,0:T(8,128)} %bitcast.177, f32[2,36,48,512]{3,2,1,0:T(8,128)} %bitcast.161, f32[8,512]{1,0:T(8,128)} %stack.94.v_ref, f32[512,1]{1,0:T(8,128)} %copy.124.mean_ref), custom_call_target="tpu_custom_call" | custom-call | tf_op jit(solution)/shard_map/weight_grad/pallas_call | solution.py:295
  389.5 44.3 %collective-permute-done = bf16[9,4,64,512]{3,2,1,0:T(8,128)(2,1)} collective-permute-done((bf16[9,4,64,512]{3,2,1,0:T(8,128)(2,1)}, bf16[9,4,64,512]{3,2,1,0:T(8,128)(2,1)}, u32[]{:S(2)}, u32[]{:S(2)}) %collective-permute-start) | collective-permute-done | bytes 2359328 | tf_op jit(solution)/shard_map/ppermute | solution.py:485
  442.0 28.7 %small_sum.9 = f32[32,512]{1,0:T(8,128)} custom-call(f32[32,512]{1,0:T(8,128)} %pad_maximum_fusion.x_ref), custom_call_target="tpu_custom_call" | custom-call | tf_op jit(solution)/shard_map/small_sum/pallas_call | solution.py:459
  485.3 27.1 %collective-permute-done.5 = bf16[9,1,64,512]{3,2,1,0:T(8,128)(2,1)S(1)} collective-permute-done((bf16[9,1,64,512]{3,2,1,0:T(8,128)(2,1)S(1)}, bf16[9,1,64,512]{3,2,1,0:T(8,128)(2,1)S(1)}, u32[]{:S(2)}, u32[]{:S(2)}) %collective-permute-start.5) | collective-permute-done | bytes 589856 | tf_op jit(solution)/shard_map/ppermute | solution.py:485
  514.0 10.8 %collective-permute-done.2 = bf16[9,1,64,512]{3,2,1,0:T(8,128)(2,1)} collective-permute-done((bf16[9,1,64,512]{3,2,1,0:T(8,128)(2,1)}, bf16[9,1,64,512]{3,2,1,0:T(8,128)(2,1)}, u32[]{:S(2)}, u32[]{:S(2)}) %collective-permute-start.2) | collective-permute-done | bytes 589856 | tf_op jit(solution)/shard_map/ppermute | solution.py:485
  541.6 10.8 %all-to-all-done = bf16[1,18,64,4,128]{4,2,1,0,3:T(8,128)(2,1)S(1)} async-done(((bf16[1,18,64,4,128]{4,2,1,0,3:T(8,128)(2,1)}), bf16[1,18,64,4,128]{4,2,1,0,3:T(8,128)(2,1)S(1)}, u32[]{:S(2)}, u32[]{:S(2)}) %all-to-all-start) | async-done | bytes 1179680 | tf_op jit(solution)/shard_map/all_to_all | solution.py:731
  555.0 10.4 %stack.107 = f32[16]{0:T(128)S(1)} concatenate(f32[1]{0:T(128)} %bitcast.45, f32[1]{0:T(128)} %bitcast.47, f32[1]{0:T(128)} %bitcast.48, f32[1]{0:T(128)} %bitcast.49, f32[1]{0:T(128)} %bitcast.47, f32[1]{0:T(128)} %bitcast.50, f32[1]{0:T(128)} %bitcast.51, f32[1]{0:T(128)} %bitcast.52, f32[1]{0:T(128)} %bitcast.48, f32[1]{0:T(128)} %bitcast.51, f32[1]{0:T(128)} %bitcast.53, ...), dimensions={0} | concatenate | bytes 128 | tf_op jit(solution)/shard_map/stack | solution.py:737
  566.6 39.5 %all-reduce.6 = (f32[4,4]{1,0:T(4,128)S(1)}, f32[256,18]{0,1:T(8,128)}, f32[4,4,512]{2,1,0:T(4,128)}, f32[4,256]{1,0:T(4,128)}, f32[4]{0:T(128)}) all-reduce(f32[4,4]{1,0:T(4,128)} %reshape.357, f32[256,18]{0,1:T(8,128)} %fusion.43, f32[4,4,512]{2,1,0:T(4,128)} %broadcast_multiply_fusion, ...), channel_id=1, replica_groups=mesh['task'=4,'dp'=8] {'task','dp'}, use_global_device_ids=true, to_apply=%region_23.24 | all-reduce | flops 13844 | bytes 110752 | tf_op jit(solution)/shard_map/psum | solution.py:736
  614.5 14.7 %all-gather.7.cloned.1.call-done = bf16[18,64,512]{2,1,0:T(8,128)(2,1)} async-done(((bf16[18,64,128]{2,1,0:T(8,128)(2,1)}), bf16[18,64,512]{2,1,0:T(8,128)(2,1)}) %all-gather.7.cloned.1.call-update) | async-done | bytes 1179664 | tf_op jit(solution)/shard_map/all_gather | solution.py:746
  629.9 66.6 %reduce-scatter.2.cloned.1.call-done = f32[1,2,64,256]{3,2,1,0:T(8,128)} async-done(((f32[1,2,512,256]{3,2,1,0:T(8,128)}), f32[1,2,64,256]{3,2,1,0:T(8,128)}) %reduce-scatter.2.cloned.1.call-update) | async-done | bytes 131088 | tf_op jit(solution)/shard_map/reduce_scatter | solution.py:725
  702.4 133.6 %all-gather.9.cloned.1.call-done.g_ref = bf16[18,512,512]{2,1,0:T(8,128)(2,1)} async-done(((bf16[18,64,512]{2,1,0:T(8,128)(2,1)}), bf16[18,512,512]{2,1,0:T(8,128)(2,1)}) %all-gather.9.cloned.1.call-update) | async-done | bytes 9437200 | tf_op jit(solution)/shard_map/all_gather | solution.py:745
  842.9 23.9 %update.1 = (f32[18,64,512]{2,1,0:T(8,128)}, f32[18,64,512]{2,1,0:T(8,128)}, f32[18,64,512]{2,1,0:T(8,128)}, f32[18,64,512]{2,1,0:T(8,128)}, bf16[18,64,512]{2,1,0:T(8,128)(2,1)}) custom-call(bf16[18,512,512]{2,1,0:T(8,128)(2,1)} %all-gather.9.cloned.1.call-done.g_ref, bf16[18,64,512]{2,1,0:T(8,128)(2,1)} %constant_dynamic-slice_fusion.1.rows_ref, ...), custom_call_target="tpu_custom_call" | custom-call | tf_op jit(solution)/shard_map/update/pallas_call | solution.py:391
  (337 shorter events, 125.6 us)
Async XLA Ops:
  7.2 222.0 %copy-start = (bf16[256,18]{0,1:T(8,128)(2,1)S(1)}, bf16[256,18]{0,1:T(8,128)(2,1)}, u32[]{:S(2)}) copy-start(bf16[256,18]{0,1:T(8,128)(2,1)} %param.46) | copy-start | bytes 27652
  7.3 90.3 %all-gather.11.cloned.1.call-start = ((), (), s32[]{:S(2)}) async-start(), calls=%async_computation.5 | async-start | bytes 5308416 | tf_op jit(solution)/shard_map/all_gather | solution.py:607
  9.8 170.0 %all-gather.13.cloned.1.call-start = ((), (), s32[]{:S(2)}) async-start(), calls=%async_computation.6 | async-start | bytes 5308416 | tf_op jit(solution)/shard_map/all_gather | solution.py:608
  294.2 90.5 %collective-permute-start.3 = (bf16[9,4,64,512]{3,2,1,0:T(8,128)(2,1)S(1)}, bf16[9,4,64,512]{3,2,1,0:T(8,128)(2,1)}, u32[]{:S(2)}, u32[]{:S(2)}) collective-permute-start(bf16[9,4,64,512]{3,2,1,0:T(8,128)(2,1)S(1)} %dynamic-slice_bitcast_fusion), channel_id=1, source_target_pairs={{0,1},{1,0},{2,3},{3,2},{4,5},{5,4},{6,7},{7,6},{8,9},{9,8},{10,11... | collective-permute-start | bytes 7077896 | tf_op jit(solution)/shard_map/ppermute | solution.py:485
  383.7 50.0 %collective-permute-start = (bf16[9,4,64,512]{3,2,1,0:T(8,128)(2,1)}, bf16[9,4,64,512]{3,2,1,0:T(8,128)(2,1)}, u32[]{:S(2)}, u32[]{:S(2)}) collective-permute-start(bf16[9,4,64,512]{3,2,1,0:T(8,128)(2,1)} %dynamic-slice_bitcast_fusion.1), channel_id=1, source_target_pairs={{0,1},{1,0},{2,3},{3,2},{4,5},{5,4},{6,7},{7,6},{8,9},{9,8},{10,11... | collective-permute-start | bytes 7077896 | tf_op jit(solution)/shard_map/ppermute | solution.py:485
  388.5 84.3 %collective-permute-start.4 = (bf16[9,2,64,512]{3,2,1,0:T(8,128)(2,1)S(1)}, bf16[9,2,64,512]{3,2,1,0:T(8,128)(2,1)}, u32[]{:S(2)}, u32[]{:S(2)}) collective-permute-start(bf16[9,2,64,512]{3,2,1,0:T(8,128)(2,1)S(1)} %fusion.11), channel_id=1, source_target_pairs={{0,2},{1,3},{2,0},{3,1},{4,6},{5,7},{6,4},{7,5},{8,10},{9,11},{10,... | collective-permute-start | bytes 3538952 | tf_op jit(solution)/shard_map/ppermute | solution.py:485
  438.7 40.1 %collective-permute-start.1 = (bf16[9,2,64,512]{3,2,1,0:T(8,128)(2,1)S(1)}, bf16[9,2,64,512]{3,2,1,0:T(8,128)(2,1)}, u32[]{:S(2)}, u32[]{:S(2)}) collective-permute-start(bf16[9,2,64,512]{3,2,1,0:T(8,128)(2,1)S(1)} %fusion.10), channel_id=1, source_target_pairs={{0,2},{1,3},{2,0},{3,1},{4,6},{5,7},{6,4},{7,5},{8,10},{9,11},{10,... | collective-permute-start | bytes 3538952 | tf_op jit(solution)/shard_map/ppermute | solution.py:485
  475.5 37.0 %collective-permute-start.5 = (bf16[9,1,64,512]{3,2,1,0:T(8,128)(2,1)S(1)}, bf16[9,1,64,512]{3,2,1,0:T(8,128)(2,1)S(1)}, u32[]{:S(2)}, u32[]{:S(2)}) collective-permute-start(bf16[9,1,64,512]{3,2,1,0:T(8,128)(2,1)S(1)} %dynamic-slice_convert_fusion.2), channel_id=1, source_target_pairs={{0,4},{1,5},{2,6},{3,7},{4,0},{5,1},{6,2},{7,3},{8,12},{9,13},{10,... | collective-permute-start | bytes 1769480 | tf_op jit(solution)/shard_map/ppermute | solution.py:485
  481.4 43.4 %collective-permute-start.2 = (bf16[9,1,64,512]{3,2,1,0:T(8,128)(2,1)}, bf16[9,1,64,512]{3,2,1,0:T(8,128)(2,1)}, u32[]{:S(2)}, u32[]{:S(2)}) collective-permute-start(bf16[9,1,64,512]{3,2,1,0:T(8,128)(2,1)} %dynamic-slice_convert_fusion.3), channel_id=1, source_target_pairs={{0,4},{1,5},{2,6},{3,7},{4,0},{5,1},{6,2},{7,3},{8,12},{9,13},{10,... | collective-permute-start | bytes 1769480 | tf_op jit(solution)/shard_map/ppermute | solution.py:485
  533.1 19.4 %all-to-all-start = ((bf16[1,18,64,4,128]{4,2,1,0,3:T(8,128)(2,1)}), bf16[1,18,64,4,128]{4,2,1,0,3:T(8,128)(2,1)S(1)}, u32[]{:S(2)}, u32[]{:S(2)}) async-start(bf16[1,18,64,4,128]{4,2,1,0,3:T(8,128)(2,1)} %copy.127), calls=%async_computation | async-start | bytes 2359296 | tf_op jit(solution)/shard_map/all_to_all | solution.py:731
  536.6 92.5 %all-gather.7.cloned.1.call-start = ((), (), s32[]{:S(2)}) async-start(), calls=%async_computation.2 | async-start | bytes 1474560 | tf_op jit(solution)/shard_map/all_gather | solution.py:746
  610.0 86.5 %reduce-scatter.2.cloned.1.call-start = ((), (), s32[]{:S(2)}) async-start(), calls=%async_computation.4 | async-start | bytes 1179648 | tf_op jit(solution)/shard_map/reduce_scatter | solution.py:725
  613.3 87.0 %copy-start.71 = (f32[4,256]{1,0:T(4,128)S(1)}, f32[4,256]{1,0:T(4,128)}, u32[]{:S(2)}) copy-start(f32[4,256]{1,0:T(4,128)} %param.53) | copy-start | bytes 12292
  613.3 87.0 %copy-start.82 = (f32[4,256]{1,0:T(4,128)S(1)}, f32[4,256]{1,0:T(4,128)}, u32[]{:S(2)}) copy-start(f32[4,256]{1,0:T(4,128)} %param.55) | copy-start | bytes 12292
  613.3 87.0 %copy-start.83 = (f32[4,256]{1,0:T(4,128)S(1)}, f32[4,256]{1,0:T(4,128)}, u32[]{:S(2)}) copy-start(f32[4,256]{1,0:T(4,128)} %param.54) | copy-start | bytes 12292
  613.3 87.0 %copy-start.84 = (f32[4,256]{1,0:T(4,128)S(1)}, f32[4,256]{1,0:T(4,128)}, u32[]{:S(2)}) copy-start(f32[4,256]{1,0:T(4,128)} %get-tuple-element.80) | copy-start | bytes 12292
  613.3 87.7 %copy-start.47 = (f32[4,512]{1,0:T(4,128)S(1)}, f32[4,512]{1,0:T(4,128)}, u32[]{:S(2)}) copy-start(f32[4,512]{1,0:T(4,128)} %param.50) | copy-start | bytes 24580
  613.3 87.7 %copy-start.73 = (f32[4,512]{1,0:T(4,128)S(1)}, f32[4,512]{1,0:T(4,128)}, u32[]{:S(2)}) copy-start(f32[4,512]{1,0:T(4,128)} %param.52) | copy-start | bytes 24580
  613.3 87.7 %copy-start.74 = (f32[4,512]{1,0:T(4,128)S(1)}, f32[4,512]{1,0:T(4,128)}, u32[]{:S(2)}) copy-start(f32[4,512]{1,0:T(4,128)} %param.51) | copy-start | bytes 24580
  613.3 88.3 %copy-start.56 = (f32[256,18]{0,1:T(8,128)S(1)}, f32[256,18]{0,1:T(8,128)}, u32[]{:S(2)}) copy-start(f32[256,18]{0,1:T(8,128)} %param.47) | copy-start | bytes 55300
  613.4 88.3 %copy-start.57 = (f32[256,18]{0,1:T(8,128)S(1)}, f32[256,18]{0,1:T(8,128)}, u32[]{:S(2)}) copy-start(f32[256,18]{0,1:T(8,128)} %param.49) | copy-start | bytes 55300
  613.4 88.3 %copy-start.58 = (f32[256,18]{0,1:T(8,128)S(1)}, f32[256,18]{0,1:T(8,128)}, u32[]{:S(2)}) copy-start(f32[256,18]{0,1:T(8,128)} %param.48) | copy-start | bytes 55300
  613.4 88.3 %copy-start.59 = (f32[256,18]{0,1:T(8,128)S(1)}, f32[256,18]{0,1:T(8,128)}, u32[]{:S(2)}) copy-start(f32[256,18]{0,1:T(8,128)} %get-tuple-element.78) | copy-start | bytes 55300
  614.5 221.5 %all-gather.9.cloned.1.call-start = ((), (), s32[]{:S(2)}) async-start(), calls=%async_computation.3 | async-start | bytes 10616832 | tf_op jit(solution)/shard_map/all_gather | solution.py:745
  (82 other events, 2040.7 us)
Sparse Core Ops, SparseCore 0:
  10.9 86.6 all-gather.10
  100.3 79.4 all-gather.12
  610.2 18.9 all-gather.6
  633.0 63.4 reduce-scatter.1
  698.8 137.0 all-gather.8

commit v2 on v1

--- a/solution.py
+++ b/solution.py
@@ -69,9 +69,12 @@
 
 
 def conv_tile(wide, weights, image, row, rows):
-    channels = weights.shape[1]
+    parts, channels, width = weights.shape[1:]
     taps = jnp.concatenate([window(wide, image, row, rows, k) for k in range(3)], axis=1)
-    return dot(taps, weights[...].reshape(9 * channels, channels))
+    full = jnp.concatenate(
+        [weights[:, part].reshape(9 * channels, width) for part in range(parts)], axis=1
+    )
+    return dot(taps, full)
 
 
 def conv_tile_back(wide, weights, image, row, rows):
@@ -80,7 +83,7 @@
         kernel_row, kernel_column = divmod(tap, 3)
         part = dot(
             window(wide, image, row, rows, 2 - kernel_row, 2 - kernel_column),
-            weights[tap],
+            jnp.concatenate([weights[tap, part] for part in range(weights.shape[1])], axis=1),
             CONTRACT_COLS,
         )
         total = part if total is None else total + part
@@ -173,6 +176,11 @@
     return pl.BlockSpec(shape, lambda g: (0,) * len(shape))
 
 
+def layer_spec(weights, layer):
+    shape = (9,) + weights.shape[1:]
+    return pl.BlockSpec(shape, lambda g: (layer, 0, 0, 0))
+
+
 def first_conv_call(x, weights):
     images, height, width, channels = x.shape
     steps, tiles, stream, rows = map_specs(*x.shape)
@@ -180,7 +188,7 @@
     return pl.pallas_call(
         functools.partial(first_kernel, steps, tiles),
         grid=(steps + tiles,),
-        in_specs=[stream, fixed(*weights.shape)],
+        in_specs=[stream, layer_spec(weights, 0)],
         out_specs=(rows, fixed(8, channels)),
         out_shape=(
             jax.ShapeDtypeStruct((pixels, channels), jnp.float32),
@@ -201,7 +209,7 @@
     return pl.pallas_call(
         functools.partial(second_kernel, steps, tiles),
         grid=(steps + tiles,),
-        in_specs=[stream, fixed(8, channels), fixed(*weights.shape)],
+        in_specs=[stream, fixed(8, channels), layer_spec(weights, 1)],
         out_specs=(rows, stream, fixed(8, channels)),
         out_shape=(
             jax.ShapeDtypeStruct((pixels, channels), jnp.float32),
@@ -348,7 +356,7 @@
     return pl.pallas_call(
         functools.partial(act_grad_kernel, steps, tiles),
         grid=(steps + tiles,),
-        in_specs=[stream, rows, fixed(8, channels), fixed(*weights.shape)],
+        in_specs=[stream, rows, fixed(8, channels), layer_spec(weights, 1)],
         out_specs=(rows, fixed(8, channels)),
         out_shape=(
             jax.ShapeDtypeStruct((pixels, channels), jnp.float32),
@@ -363,14 +371,19 @@
 
 
 def update_kernel(
-    g_ref, rows_ref, cols_ref, left_ref, right_ref, master_ref, lroot_ref,
-    rroot_ref, grad_out, left_out, right_out, master_out, copy_out,
+    place_ref, g_ref, rows_ref, cols_ref, left_ref, right_ref, master_ref, lroot_ref, rroot_ref,
+    grad_out, left_out, right_out, master_out, copy_out, gram,
 ):
-    full = g_ref[0]
-    rows = rows_ref[0]
+    parts = g_ref.shape[1]
+    shard_rows = left_ref.shape[1]
+    full = jnp.concatenate([g_ref[0, part] for part in range(parts)], axis=1)
+    rows = jnp.concatenate([rows_ref[0, part] for part in range(parts)], axis=1)
     grad_out[0] = rows.astype(jnp.float32)
     left_out[0] = 0.5 * left_ref[0] + 0.5 * dot(rows, full, CONTRACT_COLS)
-    right_out[0] = 0.5 * right_ref[0] + 0.5 * dot(cols_ref[0], full)
+    gram[...] = dot(cols_ref[0, 0], full, CONTRACT_ROWS)
+    right_out[0] = 0.5 * right_ref[0] + 0.5 * gram[
+        pl.ds(pl.multiple_of(place_ref[2], 8), shard_rows)
+    ]
     turned = dot(lroot_ref[0].astype(jnp.bfloat16), full).astype(jnp.bfloat16)
     step = dot(turned, rroot_ref[0].astype(jnp.bfloat16))
     master = master_ref[0]
@@ -381,18 +394,30 @@
 
 def update_call(owner, combined, left, right, master, lroot, rroot):
     layers, taps, shard_rows, channels = left.shape
-    count = layers * taps
-    one = pl.BlockSpec((1, shard_rows, channels), lambda g: (g, 0, 0))
-    whole = pl.BlockSpec((1, channels, channels), lambda g: (g, 0, 0))
+    count, parts, _, width = combined.shape
+    one = pl.BlockSpec((1, shard_rows, channels), lambda g, place: (g, 0, 0))
+    whole = pl.BlockSpec((1, channels, channels), lambda g, place: (g, 0, 0))
     flat = (count, shard_rows, channels)
     start = owner * shard_rows
-    rows = lax.dynamic_slice_in_dim(combined, start, shard_rows, 1)
-    cols = jnp.swapaxes(lax.dynamic_slice_in_dim(combined, start, shard_rows, 2), 1, 2)
+    place = jnp.stack([owner, start // width, lax.rem(start, width)]).astype(jnp.int32)
     outs = pl.pallas_call(
         update_kernel,
-        grid=(count,),
-        in_specs=[whole, one, one, one, one, one, one, whole],
-        out_specs=(one,) * 5,
+        grid_spec=pltpu.PrefetchScalarGridSpec(
+            num_scalar_prefetch=1,
+            grid=(count,),
+            in_specs=[
+                pl.BlockSpec((1, parts, channels, width), lambda g, place: (g, 0, 0, 0)),
+                pl.BlockSpec((1, parts, shard_rows, width), lambda g, place: (g, 0, place[0], 0)),
+                pl.BlockSpec((1, 1, channels, width), lambda g, place: (g, place[1], 0, 0)),
+                one,
+                one,
+                one,
+                one,
+                whole,
+            ],
+            out_specs=(one,) * 5,
+            scratch_shapes=[pltpu.VMEM((width, channels), jnp.float32)],
+        ),
         out_shape=tuple(
             jax.ShapeDtypeStruct(flat, kind)
             for kind in (jnp.float32, jnp.float32, jnp.float32, jnp.float32, jnp.bfloat16)
@@ -400,9 +425,10 @@
         compiler_params=PARAMS,
         name="update",
     )(
+        place,
         combined,
-        rows,
-        cols,
+        combined,
+        combined,
         left.reshape(flat),
         right.reshape(flat),
         master.reshape(flat),
@@ -410,6 +436,181 @@
         rroot.reshape(count, channels, channels),
     )
     return [out.reshape(left.shape) for out in outs]
+
+
+FAR = ("task", 2)
+CORE = ("task", 1)
+
+
+def owner_bits(members):
+    bits = []
+    bit = members // 2
+    while bit:
+        bits.append(("dp", bit))
+        bit //= 2
+    return bits
+
+
+def partner(dim):
+    axis, bit = dim
+    me = lax.axis_index(axis)
+    mine = lax.rem(me // bit, 2)
+    return mine, {axis: me + bit * (1 - 2 * mine)}
+
+
+def greet(dims):
+    barrier = pltpu.get_barrier_semaphore()
+    for dim in dims:
+        pl.semaphore_signal(
+            barrier, inc=1, device_id=partner(dim)[1], device_id_type=pl.DeviceIdType.MESH
+        )
+    pl.semaphore_wait(barrier, len(dims))
+
+
+def gather_kernel(plans, dims, split, *refs):
+    count = len(plans)
+    ins, outs = refs[:count], refs[count : 2 * count]
+    local_sem, send_sem, recv_sem = refs[2 * count :]
+    greet(dims[0])
+    task = lax.axis_index("task")
+    entries = [
+        (array, start, rows, order)
+        for array, (plan, _) in enumerate(plans)
+        for start, rows, order in plan
+    ]
+    group_of, groups = [], 0
+    for plan, width in plans:
+        group_of += [groups + i // width for i in range(len(plan))]
+        groups = group_of[-1] + 1
+
+    def held(array, start, rows, free):
+        return (pl.ds(start, rows),) + tuple(
+            slice(None) if dim in free else partner(dim)[0] for dim in dims[array]
+        )
+
+    placed = []
+    for index, (array, start, rows, order) in enumerate(entries):
+        source = ins[array].at[pl.ds(start, rows)]
+        target = held(array, start, rows, ())
+        pairs = []
+        if not split[array]:
+            pairs.append((source, target))
+        elif FAR in order:
+            column = pl.multiple_of(task * 128, 128)
+            pairs.append((ins[array].at[pl.ds(start, rows), :, pl.ds(column, 128)], target))
+        else:
+            for half in range(2):
+                column = pl.multiple_of((lax.rem(task, 2) + 2 * half) * 128, 128)
+                pairs.append(
+                    (
+                        ins[array].at[pl.ds(start, rows), :, pl.ds(column, 128)],
+                        (target[0], half) + target[2:],
+                    )
+                )
+        copies = [
+            pltpu.make_async_copy(source, outs[array].at[target], local_sem.at[index, i])
+            for i, (source, target) in enumerate(pairs)
+        ]
+        for copy in copies:
+            copy.start()
+        placed.append(copies)
+    depth = max(len(entry[3]) for entry in entries)
+    started = {}
+    for step in range(groups + depth):
+        for stage in range(depth, -1, -1):
+            for index, (array, start, rows, order) in enumerate(entries):
+                if group_of[index] != step - stage or stage > len(order):
+                    continue
+                if stage == 0:
+                    for copy in placed[index]:
+                        copy.wait()
+                else:
+                    started[index, stage - 1].wait_recv()
+                if stage < len(order):
+                    free = set(order[:stage]) | {d for d in dims[array] if d not in order}
+                    where = held(array, start, rows, free)
+                    copy = pltpu.make_async_remote_copy(
+                        src_ref=outs[array].at[where],
+                        dst_ref=outs[array].at[where],
+                        send_sem=send_sem.at[index, stage],
+                        recv_sem=recv_sem.at[index, stage],
+                        device_id=partner(order[stage])[1],
+                        device_id_type=pl.DeviceIdType.MESH,
+                    )
+                    copy.start()
+                    started[index, stage] = copy
+    for copy in started.values():
+        copy.wait_send()
+
+
+def gather(arrays, plans, dims, split, identity):
+    shapes = [
+        (x.shape[0],) + (2,) * len(d) + (x.shape[1], 128 if cut else x.shape[2])
+        for x, d, cut in zip(arrays, dims, split)
+    ]
+    entries = sum(len(plan) for plan, _ in plans)
+    depth = max(len(d) for d in dims)
+    outs = pl.pallas_call(
+        functools.partial(gather_kernel, plans, dims, split),
+        out_shape=tuple(
+            jax.ShapeDtypeStruct(shape, x.dtype) for shape, x in zip(shapes, arrays)
+        ),
+        in_specs=[pl.BlockSpec(memory_space=pl.ANY)] * len(arrays),
+        out_specs=(pl.BlockSpec(memory_space=pl.ANY),) * len(arrays),
+        scratch_shapes=[
+            pltpu.SemaphoreType.DMA((entries, 2)),
+            pltpu.SemaphoreType.DMA((entries, depth)),
+            pltpu.SemaphoreType.DMA((entries, depth)),
+        ],
+        compiler_params=pltpu.CompilerParams(collective_id=identity, has_side_effects=True),
+        name="gather",
+    )(*arrays)
+    return outs
+
+
+def spread(orders, taps, width):
+    rows = taps // len(orders)
+    return [(i * rows, rows, order) for i, order in enumerate(orders)], width
+
+
+def gather_weights(trunk, head, identity):
+    members = lax.axis_size("dp")
+    bits = owner_bits(members)
+    quarters = tuple(bits) + (FAR, CORE)
+    halves = tuple(bits) + (CORE,)
+    layers, taps, shard_rows, channels = trunk.shape
+    trunk_plan = spread([quarters, halves, quarters] * 6, layers * taps, 6)
+    head_plan = spread([tuple(bits)], 2, 1)
+    full, heads = gather(
+        [trunk.reshape(layers * taps, shard_rows, channels), head[0]],
+        [trunk_plan, head_plan],
+        [[FAR, CORE] + bits, bits],
+        [True, False],
+        identity,
+    )
+    return (
+        full.reshape(layers * taps, TASKS, channels, 128),
+        heads.reshape(2, channels, head.shape[3]),
+    )
+
+
+def gather_combined(quarter, identity):
+    members = lax.axis_size("dp")
+    bits = owner_bits(members)
+    last = bits[-1:]
+    plain = tuple(bits) + (FAR, CORE)
+    other = tuple(bits[:-1]) + (FAR,) + tuple(last) + (CORE,)
+    early = tuple(last) + (FAR,) + tuple(bits[:-1]) + (CORE,)
+    first = (FAR,) + tuple(last) + tuple(bits[:-1]) + (CORE,)
+    taps, shard_rows, width = quarter.shape
+    (full,) = gather(
+        [quarter],
+        [spread([plain, other, plain, other, early, first] * 3, taps, 6)],
+        [[FAR, CORE] + bits],
+        [False],
+        identity,
+    )
+    return full.reshape(taps, TASKS, members * shard_rows, width)
 
 
 def small_sum_kernel(members, x_ref, out_ref, slots, send_sem, recv_sem):
@@ -604,21 +805,19 @@
     pixels = jnp.array(images * feature_rows * feature_columns * lax.axis_size("dp"), jnp.float32)
     task_index = lax.axis_index("task")
     owner_index = lax.axis_index("dp")
-    trunk_first = lax.all_gather(trunk_copy[0], "dp", axis=1, tiled=True)
-    trunk_second = lax.all_gather(trunk_copy[1], "dp", axis=1, tiled=True)
-    head_full = lax.all_gather(head_copy, "dp", axis=2, tiled=True)
+    trunk_full, head_full = gather_weights(trunk_copy, head_copy, 5)
     pixel_info = pixel_data(
         labels, depth_mask, depth_target, normal_target, scene_ids, task_weights
     )
     local_valid = jnp.sum(pixel_info[1])
-    first_conv, first_sums = first_conv_call(features, trunk_first)
+    first_conv, first_sums = first_conv_call(features, trunk_full)
     first_totals = small_sum(
         pad_rows([first_sums[:3], jnp.full((1, channels), local_valid)], 8), 0
     )
     valid_count = first_totals[3, 0]
     first_norm = norm_vectors(first_totals, trunk_gains[0], trunk_gains[1], pixels)
     second_conv, first_act, second_sums = second_conv_call(
-        first_conv, stack_vectors(first_norm), trunk_second, features.shape
+        first_conv, stack_vectors(first_norm), trunk_full, features.shape
     )
     second_totals = small_sum(second_sums, 1)
     second_norm = norm_vectors(second_totals, trunk_gains[2], trunk_gains[3], pixels)
@@ -632,12 +831,12 @@
     )
     selector = (jnp.arange(TASKS) == task_index).astype(jnp.float32)
     own_bias = jnp.dot(selector, head_bias, precision=PRECISE)
-    head_pre = jnp.dot(trunk_out, head_full[0, 0], preferred_element_type=jnp.float32).reshape(
+    head_pre = jnp.dot(trunk_out, head_full[0], preferred_element_type=jnp.float32).reshape(
         images, -1, BRANCH_WIDTH
     )
     head_pre = (
         head_pre
-        + jnp.dot(pooled, head_full[0, 1], preferred_element_type=jnp.float32)[:, None, :]
+        + jnp.dot(pooled, head_full[1], preferred_element_type=jnp.float32)[:, None, :]
         + own_bias
     )
     head_pre = head_pre.reshape(-1, BRANCH_WIDTH)
@@ -652,12 +851,13 @@
     per_image = jnp.sum(pre_grad.reshape(images, -1, BRANCH_WIDTH), axis=1, dtype=jnp.float32)
     input_grad = dot(trunk_out, pre_grad, CONTRACT_ROWS)
     pool_grad = jnp.dot(pooled.astype(jnp.float32).T, per_image, precision=PRECISE)
-    pooled_back = jnp.dot(per_image, head_full[0, 1].astype(jnp.float32).T, precision=PRECISE)
-    out_back = dot(pre_grad, head_full[0, 0], CONTRACT_COLS)
+    pooled_back = jnp.dot(per_image, head_full[1].astype(jnp.float32).T, precision=PRECISE)
+    out_back = dot(pre_grad, head_full[0], CONTRACT_COLS)
     out_back = (
         out_back.reshape(images, -1, channels)
         + pooled_back[:, None, :] / (feature_rows * feature_columns)
     ).reshape(-1, channels)
+    head_sum = scatter_sum(jnp.concatenate([input_grad, pool_grad], axis=1)[None])
     second_up = out_back * silu_slope(residual_in)
     second_back_sums = small_sum(
         pad_rows(
@@ -680,7 +880,7 @@
     )
     second_sum = scatter_sum(second_weight)
     first_up, first_up_sums = act_grad_call(
-        second_back, first_conv, stack_vectors(first_norm), trunk_second
+        second_back, first_conv, stack_vectors(first_norm), trunk_full
     )
     first_back_sums = small_sum(first_up_sums, 3)[:2]
     first_mean = first_totals[2] / pixels
@@ -698,7 +898,6 @@
     shard_rows = trunk_copy.shape[2]
     own_means = lax.dynamic_slice_in_dim(means, owner_index * shard_rows, shard_rows, 1)
     removed = (own_means[:, None, :, None] * edges[:, :9]).reshape(18, shard_rows, channels)
-    head_grad = jnp.stack([input_grad, pool_grad])[None]
     leading = (owner_index == 0).astype(jnp.float32)
     gains_part = (
         selector[:, None, None]
@@ -722,7 +921,7 @@
         [jnp.full((CLASSES,), divisor[0]), divisor[1:2], jnp.full((3,), divisor[2]), divisor[3:4]]
     )
     out_total = out_sum / column_divisor[None, :]
-    head_rows = lax.psum_scatter(head_grad, "dp", scatter_dimension=2, tiled=True)
+    head_rows = jnp.stack(jnp.split(head_sum[0], 2, axis=1))[None]
     own_scaled = (
         (jnp.concatenate([first_sum, second_sum]) + removed) / own_divisor
     ).astype(jnp.bfloat16)
@@ -742,9 +941,7 @@
     mixing = combine_weights(pair_products, conflict)
     quarter = jnp.sum(mixing[:, None, None] * scaled, axis=0).astype(jnp.bfloat16)
     quarter = quarter.reshape(taps, shard_rows, channels // TASKS)
-    combined = lax.all_gather(
-        lax.all_gather(quarter, "task", axis=2, tiled=True), "dp", axis=1, tiled=True
-    )
+    combined = gather_combined(quarter, 6)
     grad_rows, left_new, right_new, master_new, copy_new = update_call(
         owner_index, combined, trunk_left, trunk_right, trunk_master, left_root, right_root
     )

time: 882 us -> 645 us (0.73)
  waiting for transfers between devices: 392 us -> 81.2 us
  Pallas kernels: 248 us -> 367 us
  blocking collectives: 76.1 us -> 40.3 us
  between operations: 15.5 us -> 2.36 us
    all_gather x4 -> x0, waiting for transfers between devices: 232 us -> none  [the longest x1 134 us: body(): lax.all_gather(lax.all_gather(quarter, 'task', axis=2, tiled=True), 'dp',...]
    pallas_call x1 -> x3, Pallas kernels: 23.9 us -> 141 us  [the longest x2 117 us: gather(): pl.pallas_call(functools.partial(gather_kernel, plans, dims, split), out_...]
    reduce_scatter x1 -> x0, waiting for transfers between devices: 66.6 us -> none  [body(): lax.psum_scatter(head_grad, 'dp', scatter_dimension=2, tiled=True)]
    all_gather x1 -> x0, blocking collectives: 36.6 us -> none  [body(): head_full = lax.all_gather(head_copy, 'dp', axis=2, tiled=True)]
    ppermute x6 -> x9, waiting for transfers between devices: 82.3 us -> 73.3 us  [scatter_sum(): lax.ppermute(other.astype(jnp.bfloat16), 'dp', [(i, i ^ bit) for i in ran...]
  transfers between devices with their start and end apart: 12 -> 10, of which waited for: 9 -> 5; matrix products, arithmetic and copies ran while one was open for 6% -> 7% of each run, Pallas kernels for 17% -> 17%
where the time goes in v2:
time: 645 us; the launch traced here: 635 us
  Pallas kernels  367 us (57%)
  waiting for transfers between devices  81.2 us (13%)
  other arithmetic  66.7 us (10%)
  local copies, waits for them, and re-layouts  54.6 us (8%)
  blocking collectives  40.3 us (6%)
  starting transfers between devices  13.3 us (2%)
  matrix products  9.54 us (1%)
    pallas_call x2, Pallas kernels, gather(): pl.pallas_call(functools.partial(gather_kernel, plans, dims, split), out_...  117 us
    pallas_call x5, Pallas kernels, small_sum(): pl.pallas_call(functools.partial(small_sum_kernel, members), out_shape=ja...  77.2 us
    ppermute x9, waiting for transfers between devices, scatter_sum(): lax.ppermute(other.astype(jnp.bfloat16), 'dp', [(i, i ^ bit) for i in ran...  73.3 us
    pallas_call x2, Pallas kernels, weight_grad_call(): pl.pallas_call(functools.partial(weight_kernel, steps, keep_back), grid=(...  65 us
    psum x1, blocking collectives, body(): lax.psum(jnp.stack([products[min(i, j), max(i, j)] for i in range(TASKS)...  40.3 us
    pallas_call x1, Pallas kernels, second_conv_call(): pl.pallas_call(functools.partial(second_kernel, steps, tiles), grid=(step...  28.9 us
    pallas_call x1, Pallas kernels, act_grad_call(): pl.pallas_call(functools.partial(act_grad_kernel, steps, tiles), grid=(st...  28.8 us
    pallas_call x1, Pallas kernels, first_conv_call(): pl.pallas_call(functools.partial(first_kernel, steps, tiles), grid=(steps...  26.5 us
  transfers between devices with their start and end apart: 10, of which 5 were waited for; matrix products, arithmetic and copies ran while one was open for 7% of the time, Pallas kernels for 17%

profile of v2, /device:TPU:0, one launch (start us, length us, event | category | flops | bytes accessed | tf_op | source)
XLA Modules:
  0.0 635.4 jit_solution(15764646772226607685)
XLA Ops:
  20.4 62.7 %gather.8 = (bf16[18,2,2,2,2,2,64,128]{7,6,5,4,3,2,1,0:T(8,128)(2,1)}, bf16[2,2,2,2,64,256]{5,4,3,2,1,0:T(8,128)(2,1)}) custom-call(bf16[18,64,512]{2,1,0:T(8,128)(2,1)} %bitcast.210, bf16[2,64,256]{2,1,0:T(8,128)(2,1)} %bitcast.215), custom_call_target="tpu_custom_call" | custom-call | tf_op jit(solution)/shard_map/gather/pallas_call | solution.py:553
  84.9 26.5 %first_conv.1 = (f32[3456,512]{1,0:T(8,128)}, f32[8,512]{1,0:T(8,128)}) custom-call(bf16[2,36,48,512]{3,2,1,0:T(8,128)(2,1)} %x_ref.3, bf16[18,4,512,128]{3,2,1,0:T(8,128)(2,1)} %bitcast.175), custom_call_target="tpu_custom_call" | custom-call | tf_op jit(solution)/shard_map/first_conv/pallas_call | solution.py:188
  112.8 9.5 %small_sum.5 = f32[8,512]{1,0:T(8,128)} custom-call(f32[8,512]{1,0:T(8,128)} %maximum_maximum_fusion.x_ref), custom_call_target="tpu_custom_call" | custom-call | tf_op jit(solution)/shard_map/small_sum/pallas_call | solution.py:660
  124.4 28.9 %second_conv.1 = (f32[3456,512]{1,0:T(8,128)}, bf16[2,36,48,512]{3,2,1,0:T(8,128)(2,1)}, f32[8,512]{1,0:T(8,128)}) custom-call(f32[2,36,48,512]{3,2,1,0:T(8,128)} %bitcast.178, f32[8,512]{1,0:T(8,128)} %maximum_maximum_fusion.1.v_ref, bf16[18,4,512,128]{3,2,1,0:T(8,128)(2,1)} %bitcast.176), custom_call_target="tpu_custom_call" | custom-call | tf_op jit(solution)/shard_map/second_conv/pallas_call | solution.py:209
  153.4 8.7 %small_sum.6 = f32[8,512]{1,0:T(8,128)} custom-call(f32[8,512]{1,0:T(8,128)} %get-tuple-element.45.x_ref), custom_call_target="tpu_custom_call" | custom-call | tf_op jit(solution)/shard_map/small_sum/pallas_call | solution.py:660
  165.1 5.0 multiply_convert_fusion
  187.3 6.8 %fusion.47 = (f32[512]{0:T(512)S(1)}, f32[512]{0:T(512)S(1)}, f32[3456,512]{1,0:T(8,128)}) fusion(f32[512]{0:T(512)S(1)} %bitcast.217, f32[3456,512]{1,0:T(8,128)S(1)} %bitcast.182, f32[512]{0:T(512)S(1)} %bitcast.219, bf16[2,36,48,512]{3,2,1,0:T(8,128)(2,1)S(1)} %copy-done.3, f32[512]{0:T(512)S(1)} %bitcast.223, f32[512]{0:T(512)S(1)} %bitcast.221, ...), kind=kLoop, calls=%fused_computation.185 | loop fusion | flops 30080000 | bytes 24784896 | tf_op jit(solution)/shard_map/reduce_sum | solution.py:865
  194.7 8.8 %small_sum.7 = f32[8,512]{1,0:T(8,128)} custom-call(f32[8,512]{1,0:T(8,128)} %maximum_maximum_fusion.2.x_ref), custom_call_target="tpu_custom_call" | custom-call | tf_op jit(solution)/shard_map/small_sum/pallas_call | solution.py:660
  205.6 32.8 %weight_grad.2 = (bf16[9,512,512]{2,1,0:T(8,128)(2,1)}, f32[16,512]{1,0:T(8,128)}, bf16[2,36,48,512]{3,2,1,0:T(8,128)(2,1)}) custom-call(bf16[2,36,48,512]{3,2,1,0:T(8,128)(2,1)} %get-tuple-element.43.x_ref, f32[2,36,48,512]{3,2,1,0:T(8,128)} %bitcast.183, f32[2,36,48,512]{3,2,1,0:T(8,128)} %bitcast.180, f32[8,512]{1,0:T(8,128)} %stack.109.v_ref, ...), custom_call_target="tpu_custom_call" | custom-call | tf_op jit(solution)/shard_map/weight_grad/pallas_call | solution.py:303
  244.3 28.8 %act_grad.1 = (f32[3456,512]{1,0:T(8,128)}, f32[8,512]{1,0:T(8,128)}) custom-call(bf16[2,36,48,512]{3,2,1,0:T(8,128)(2,1)} %get-tuple-element.47.back_ref, f32[3456,512]{1,0:T(8,128)} %get-tuple-element.41.y_ref, f32[8,512]{1,0:T(8,128)} %maximum_maximum_fusion.1.v_ref, bf16[18,4,512,128]{3,2,1,0:T(8,128)(2,1)} %bitcast.177), custom_call_target="tpu_custom_call" | custom-call | tf_op jit(solution)/shard_map/act_grad/pallas_call | solution.py:356
  273.0 21.4 %small_sum.8 = f32[8,512]{1,0:T(8,128)} custom-call(f32[8,512]{1,0:T(8,128)} %get-tuple-element.49.x_ref), custom_call_target="tpu_custom_call" | custom-call | tf_op jit(solution)/shard_map/small_sum/pallas_call | solution.py:660
  295.8 32.1 %weight_grad.3 = (bf16[9,512,512]{2,1,0:T(8,128)(2,1)}, f32[16,512]{1,0:T(8,128)}) custom-call(bf16[2,36,48,512]{3,2,1,0:T(8,128)(2,1)} %x_ref.3, f32[2,36,48,512]{3,2,1,0:T(8,128)} %bitcast.193, f32[2,36,48,512]{3,2,1,0:T(8,128)} %bitcast.179, f32[8,512]{1,0:T(8,128)} %stack.110.v_ref, f32[512,1]{1,0:T(8,128)} %copy.118.mean_ref), custom_call_target="tpu_custom_call" | custom-call | tf_op jit(solution)/shard_map/weight_grad/pallas_call | solution.py:303
  349.7 34.5 %collective-permute-done = bf16[9,4,64,512]{3,2,1,0:T(8,128)(2,1)} collective-permute-done((bf16[9,4,64,512]{3,2,1,0:T(8,128)(2,1)}, bf16[9,4,64,512]{3,2,1,0:T(8,128)(2,1)}, u32[]{:S(2)}, u32[]{:S(2)}) %collective-permute-start) | collective-permute-done | bytes 2359328 | tf_op jit(solution)/shard_map/ppermute | solution.py:686
  391.6 28.8 %small_sum.9 = f32[32,512]{1,0:T(8,128)} custom-call(f32[32,512]{1,0:T(8,128)} %pad_maximum_fusion.1.x_ref), custom_call_target="tpu_custom_call" | custom-call | tf_op jit(solution)/shard_map/small_sum/pallas_call | solution.py:660
  434.9 23.9 %collective-permute-done.5 = bf16[9,1,64,512]{3,2,1,0:T(8,128)(2,1)S(1)} collective-permute-done((bf16[9,1,64,512]{3,2,1,0:T(8,128)(2,1)S(1)}, bf16[9,1,64,512]{3,2,1,0:T(8,128)(2,1)S(1)}, u32[]{:S(2)}, u32[]{:S(2)}) %collective-permute-start.5) | collective-permute-done | bytes 589856 | tf_op jit(solution)/shard_map/ppermute | solution.py:686
  460.4 10.8 %collective-permute-done.2 = bf16[9,1,64,512]{3,2,1,0:T(8,128)(2,1)} collective-permute-done((bf16[9,1,64,512]{3,2,1,0:T(8,128)(2,1)}, bf16[9,1,64,512]{3,2,1,0:T(8,128)(2,1)}, u32[]{:S(2)}, u32[]{:S(2)}) %collective-permute-start.2) | collective-permute-done | bytes 589856 | tf_op jit(solution)/shard_map/ppermute | solution.py:686
  472.9 3.9 fusion.9
  478.1 3.5 all-to-all-start
  485.5 4.1 collective-permute-done.8
  489.7 7.8 %all-to-all-done = bf16[1,18,64,4,128]{4,2,1,0,3:T(8,128)(2,1)S(1)} async-done(((bf16[1,18,64,4,128]{4,2,1,0,3:T(8,128)(2,1)}), bf16[1,18,64,4,128]{4,2,1,0,3:T(8,128)(2,1)S(1)}, u32[]{:S(2)}, u32[]{:S(2)}) %all-to-all-start) | async-done | bytes 1179680 | tf_op jit(solution)/shard_map/all_to_all | solution.py:930
  499.0 10.4 %stack.123 = f32[16]{0:T(128)S(1)} concatenate(f32[1]{0:T(128)} %bitcast.49, f32[1]{0:T(128)} %bitcast.51, f32[1]{0:T(128)} %bitcast.52, f32[1]{0:T(128)} %bitcast.53, f32[1]{0:T(128)} %bitcast.51, f32[1]{0:T(128)} %bitcast.54, f32[1]{0:T(128)} %bitcast.55, f32[1]{0:T(128)} %bitcast.56, f32[1]{0:T(128)} %bitcast.52, f32[1]{0:T(128)} %bitcast.55, f32[1]{0:T(128)} %bitcast.57, ...), dimensions={0} | concatenate | bytes 128 | tf_op jit(solution)/shard_map/stack | solution.py:936
  511.0 40.3 %all-reduce.6 = (f32[4,4]{1,0:T(4,128)S(1)}, f32[256,18]{0,1:T(8,128)S(1)}, f32[4,4,512]{2,1,0:T(4,128)S(1)}, f32[4,256]{1,0:T(4,128)S(1)}, f32[4]{0:T(128)S(1)}) all-reduce(f32[4,4]{1,0:T(4,128)S(1)} %reshape.465, f32[256,18]{0,1:T(8,128)S(1)} %copy-done.38, ...), channel_id=1, replica_groups=mesh['task'=4,'dp'=8] {'task','dp'}, use_global_device_ids=true, to_apply=%region_23.24 | all-reduce | flops 13844 | bytes 110752 | tf_op jit(solution)/shard_map/psum | solution.py:935
  554.4 54.0 %gather.9 = bf16[18,2,2,2,2,2,64,128]{7,6,5,4,3,2,1,0:T(8,128)(2,1)} custom-call(bf16[18,64,128]{2,1,0:T(8,128)(2,1)} %fusion.7.refs_0_), custom_call_target="tpu_custom_call" | custom-call | tf_op jit(solution)/shard_map/gather/pallas_call | solution.py:553
  610.6 24.3 %update.1 = (f32[18,64,512]{2,1,0:T(8,128)}, f32[18,64,512]{2,1,0:T(8,128)}, f32[18,64,512]{2,1,0:T(8,128)}, f32[18,64,512]{2,1,0:T(8,128)}, bf16[18,64,512]{2,1,0:T(8,128)(2,1)}) custom-call(s32[3]{0:T(128)} %pad_add_fusion.place_ref, bf16[18,4,512,128]{3,2,1,0:T(8,128)(2,1)} %bitcast.172, bf16[18,4,512,128]{3,2,1,0:T(8,128)(2,1)} %bitcast.173, ...), custom_call_target="tpu_custom_call" | custom-call | tf_op jit(solution)/shard_map/update/pallas_call | solution.py:403
  (319 shorter events, 114.5 us)
Async XLA Ops:
  0.7 173.9 %copy-start = (bf16[256,18]{0,1:T(8,128)(2,1)S(1)}, bf16[256,18]{0,1:T(8,128)(2,1)}, u32[]{:S(2)}) copy-start(bf16[256,18]{0,1:T(8,128)(2,1)} %param.46) | copy-start | bytes 27652
  241.7 102.2 %collective-permute-start.3 = (bf16[9,4,64,512]{3,2,1,0:T(8,128)(2,1)}, bf16[9,4,64,512]{3,2,1,0:T(8,128)(2,1)}, u32[]{:S(2)}, u32[]{:S(2)}) collective-permute-start(bf16[9,4,64,512]{3,2,1,0:T(8,128)(2,1)} %dynamic-slice_bitcast_fusion), channel_id=1, source_target_pairs={{0,1},{1,0},{2,3},{3,2},{4,5},{5,4},{6,7},{7,6},{8,9},{9,8},{10,11... | collective-permute-start | bytes 7077896 | tf_op jit(solution)/shard_map/ppermute | solution.py:686
  331.5 52.7 %collective-permute-start = (bf16[9,4,64,512]{3,2,1,0:T(8,128)(2,1)}, bf16[9,4,64,512]{3,2,1,0:T(8,128)(2,1)}, u32[]{:S(2)}, u32[]{:S(2)}) collective-permute-start(bf16[9,4,64,512]{3,2,1,0:T(8,128)(2,1)} %dynamic-slice_bitcast_fusion.1), channel_id=1, source_target_pairs={{0,1},{1,0},{2,3},{3,2},{4,5},{5,4},{6,7},{7,6},{8,9},{9,8},{10,11... | collective-permute-start | bytes 7077896 | tf_op jit(solution)/shard_map/ppermute | solution.py:686
  336.0 95.9 %collective-permute-start.6 = (bf16[1,4,64,512]{3,2,1,0:T(8,128)(2,1)}, bf16[1,4,64,512]{3,2,1,0:T(8,128)(2,1)}, u32[]{:S(2)}, u32[]{:S(2)}) collective-permute-start(bf16[1,4,64,512]{3,2,1,0:T(8,128)(2,1)} %fusion.12), channel_id=1, source_target_pairs={{0,1},{1,0},{2,3},{3,2},{4,5},{5,4},{6,7},{7,6},{8,9},{9,8},{10,11... | collective-permute-start | bytes 786440 | tf_op jit(solution)/shard_map/ppermute | solution.py:686
  348.6 73.3 %copy-start.64 = (f32[4]{0:T(128)S(1)}, f32[4]{0:T(128)}, u32[]{:S(2)}) copy-start(f32[4]{0:T(128)} %copy-done.63) | copy-start | bytes 52
  348.6 73.3 %copy-start.75 = (f32[256]{0:T(256)S(1)}, f32[256]{0:T(256)}, u32[]{:S(2)}) copy-start(f32[256]{0:T(256)} %get-tuple-element.143) | copy-start | bytes 3076
  348.6 74.0 %copy-start.7 = (bf16[3456,256]{1,0:T(8,128)(2,1)S(1)}, bf16[3456,256]{1,0:T(8,128)(2,1)}, u32[]{:S(2)}) copy-start(bf16[3456,256]{1,0:T(8,128)(2,1)} %copy-done.6) | copy-start | bytes 5308420
  348.6 74.0 %copy-start.15 = (f32[3456,13]{0,1:T(8,128)S(1)}, f32[3456,13]{0,1:T(8,128)}, u32[]{:S(2)}) copy-start(f32[3456,13]{0,1:T(8,128)} %copy-done.14) | copy-start | bytes 539140
  348.6 74.0 %copy-start.20 = (f32[3456,3]{0,1:T(4,128)S(1)}, f32[3456,3]{0,1:T(4,128)}, u32[]{:S(2)}) copy-start(f32[3456,3]{0,1:T(4,128)} %copy-done.19) | copy-start | bytes 124420
  348.7 74.0 %copy-start.35 = (f32[3456,1]{0,1:T(1,128)S(1)}, f32[3456,1]{0,1:T(1,128)}, u32[]{:S(2)}) copy-start(f32[3456,1]{0,1:T(1,128)} %copy-done.34) | copy-start | bytes 41476
  348.7 74.0 %copy-start.37 = (f32[3456,1]{0,1:T(1,128)S(1)}, f32[3456,1]{0,1:T(1,128)}, u32[]{:S(2)}) copy-start(f32[3456,1]{0,1:T(1,128)} %copy-done.36) | copy-start | bytes 41476
  348.7 75.0 %collective-permute-start.4 = (bf16[9,2,64,512]{3,2,1,0:T(8,128)(2,1)}, bf16[9,2,64,512]{3,2,1,0:T(8,128)(2,1)}, u32[]{:S(2)}, u32[]{:S(2)}) collective-permute-start(bf16[9,2,64,512]{3,2,1,0:T(8,128)(2,1)} %fusion.11), channel_id=1, source_target_pairs={{0,2},{1,3},{2,0},{3,1},{4,6},{5,7},{6,4},{7,5},{8,10},{9,11},{10,... | collective-permute-start | bytes 3538952 | tf_op jit(solution)/shard_map/ppermute | solution.py:686
  390.1 38.4 %collective-permute-start.1 = (bf16[9,2,64,512]{3,2,1,0:T(8,128)(2,1)}, bf16[9,2,64,512]{3,2,1,0:T(8,128)(2,1)}, u32[]{:S(2)}, u32[]{:S(2)}) collective-permute-start(bf16[9,2,64,512]{3,2,1,0:T(8,128)(2,1)} %fusion.10), channel_id=1, source_target_pairs={{0,2},{1,3},{2,0},{3,1},{4,6},{5,7},{6,4},{7,5},{8,10},{9,11},{10,... | collective-permute-start | bytes 3538952 | tf_op jit(solution)/shard_map/ppermute | solution.py:686
  426.3 32.5 %collective-permute-start.5 = (bf16[9,1,64,512]{3,2,1,0:T(8,128)(2,1)S(1)}, bf16[9,1,64,512]{3,2,1,0:T(8,128)(2,1)S(1)}, u32[]{:S(2)}, u32[]{:S(2)}) collective-permute-start(bf16[9,1,64,512]{3,2,1,0:T(8,128)(2,1)S(1)} %dynamic-slice_convert_fusion.2), channel_id=1, source_target_pairs={{0,4},{1,5},{2,6},{3,7},{4,0},{5,1},{6,2},{7,3},{8,12},{9,13},{10,... | collective-permute-start | bytes 1769480 | tf_op jit(solution)/shard_map/ppermute | solution.py:686
  431.2 40.1 %collective-permute-start.2 = (bf16[9,1,64,512]{3,2,1,0:T(8,128)(2,1)}, bf16[9,1,64,512]{3,2,1,0:T(8,128)(2,1)}, u32[]{:S(2)}, u32[]{:S(2)}) collective-permute-start(bf16[9,1,64,512]{3,2,1,0:T(8,128)(2,1)} %dynamic-slice_convert_fusion.3), channel_id=1, source_target_pairs={{0,4},{1,5},{2,6},{3,7},{4,0},{5,1},{6,2},{7,3},{8,12},{9,13},{10,... | collective-permute-start | bytes 1769480 | tf_op jit(solution)/shard_map/ppermute | solution.py:686
  433.7 48.0 %collective-permute-start.7 = (bf16[1,2,64,512]{3,2,1,0:T(8,128)(2,1)}, bf16[1,2,64,512]{3,2,1,0:T(8,128)(2,1)}, u32[]{:S(2)}, u32[]{:S(2)}) collective-permute-start(bf16[1,2,64,512]{3,2,1,0:T(8,128)(2,1)} %fusion.15), channel_id=1, source_target_pairs={{0,2},{1,3},{2,0},{3,1},{4,6},{5,7},{6,4},{7,5},{8,10},{9,11},{10,... | collective-permute-start | bytes 393224 | tf_op jit(solution)/shard_map/ppermute | solution.py:686
  478.1 19.4 %all-to-all-start = ((bf16[1,18,64,4,128]{4,2,1,0,3:T(8,128)(2,1)}), bf16[1,18,64,4,128]{4,2,1,0,3:T(8,128)(2,1)S(1)}, u32[]{:S(2)}, u32[]{:S(2)}) async-start(bf16[1,18,64,4,128]{4,2,1,0,3:T(8,128)(2,1)} %copy.121), calls=%async_computation | async-start | bytes 2359296 | tf_op jit(solution)/shard_map/all_to_all | solution.py:930
  482.8 6.8 %collective-permute-start.8 = (bf16[1,1,64,512]{3,2,1,0:T(8,128)(2,1)S(1)}, bf16[1,1,64,512]{3,2,1,0:T(8,128)(2,1)S(1)}, u32[]{:S(2)}, u32[]{:S(2)}) collective-permute-start(bf16[1,1,64,512]{3,2,1,0:T(8,128)(2,1)S(1)} %dynamic-slice_convert_fusion.6), channel_id=1, source_target_pairs={{0,4},{1,5},{2,6},{3,7},{4,0},{5,1},{6,2},{7,3},{8,12},{9,13},{10,... | collective-permute-start | bytes 196616 | tf_op jit(solution)/shard_map/ppermute | solution.py:686
  489.6 61.7 %copy-start.68 = (s32[4]{0:T(128)S(1)}, s32[4]{0:T(128)}, u32[]{:S(2)}) copy-start(s32[4]{0:T(128)} %or_bitcast_fusion) | copy-start | bytes 52
  489.6 62.4 %copy-start.79 = (s32[4,4]{1,0:T(4,128)S(1)}, s32[4,4]{1,0:T(4,128)}, u32[]{:S(2)}) copy-start(s32[4,4]{1,0:T(4,128)} %param.35) | copy-start | bytes 196
  551.4 57.0 %copy-start.2 = (f32[4,4]{1,0:T(4,128)}, f32[4,4]{1,0:T(4,128)S(1)}, u32[]{:S(2)}) copy-start(f32[4,4]{1,0:T(4,128)S(1)} %get-tuple-element.81) | copy-start | bytes 196
  554.4 55.5 %copy-start.54 = (f32[256,18]{0,1:T(8,128)S(1)}, f32[256,18]{0,1:T(8,128)}, u32[]{:S(2)}) copy-start(f32[256,18]{0,1:T(8,128)} %param.47) | copy-start | bytes 55300
  554.4 55.5 %copy-start.55 = (f32[256,18]{0,1:T(8,128)S(1)}, f32[256,18]{0,1:T(8,128)}, u32[]{:S(2)}) copy-start(f32[256,18]{0,1:T(8,128)} %param.49) | copy-start | bytes 55300
  554.4 55.5 %copy-start.56 = (f32[256,18]{0,1:T(8,128)S(1)}, f32[256,18]{0,1:T(8,128)}, u32[]{:S(2)}) copy-start(f32[256,18]{0,1:T(8,128)} %param.48) | copy-start | bytes 55300
  (72 other events, 1099.9 us)
